TPU v7x, 512 devices: a whole 4x4x16 slice. The times are simulated.
512 devices in a mesh: frac: 8 (over y, core), tile: 64 (over x, z).
Axes of the slice: x: 4, y: 4, z: 16, core: 2. Of those that a mesh axis runs over, the one named last changes fastest.
Arguments:
- frames: bfloat16 [8, 2048, 4096], P('frac', 'tile'), may hold values from -6 to 6
- gain_reference: bfloat16 [2048, 4096], P('tile'), may hold values from 0.5 to 2
- defect_pixel: int32 [32768], P('tile'), may hold values from 0 to 131071, as said below
- defect_offset: int32 [32768], P('tile'), may hold values from -4 to 4, as said below
- fraction_group: int32 [8], replicated, may hold values from 0 to 7
- exposure_filter: float32 [8, 512, 512], P(None, 'tile'), may hold values from 0.25 to 1
Outputs:
- summed_image: float32 [32, 512, 512], P('frac', 'tile')
Inputs may be any that keep to these rules, and one draw needn't show every extreme that they name: `defect_pixel`: within one index of tile the defective pixels are distinct. `defect_offset`: never 0; every fill source lies inside the frame.
All inputs are finite; a program needn't handle non-finite values.
Results may differ from a plain program's by a relative error of at most 0.0065.
Values may be sent and summed in bfloat16 or wider, within the bound.
No kernel may reach another device: no remote copies, remote signals or barrier semaphores. Data moves between devices by JAX's collectives and lax.ppermute only.
A program may use at most 64 MiB of HBM per device.

v0:
```python
import jax
import jax.numpy as jnp
import ml_dtypes
import numpy as np
from jax import lax
from jax.experimental import pallas as pl
from jax.experimental.pallas import tpu as pltpu
from jax.sharding import PartitionSpec as P

N = 512
RIM = 4
TILES = 64
FRACS = 8
COLS = 8
ROWS = 32
WIDTH = N * COLS
F32 = jnp.float32
BF16 = jnp.bfloat16
VMEM_LIMIT = 48 * 1024 * 1024


def wave(a, b):
    angle = (2.0 * np.pi / N) * (np.multiply.outer(a, b) % N)
    return np.cos(angle), np.sin(angle)


def owned_columns():
    tile = np.arange(TILES)[:, None]
    return 8 * tile + np.arange(4)[None, :] + (tile >= TILES // 2)


def forward_columns_table():
    cosine, sine = wave(owned_columns(), np.arange(N))
    table = np.stack([cosine, -sine], axis=1)
    table[0, 1, 0] = 1.0 - 2.0 * (np.arange(N) % 2)
    return table.reshape(N, N).astype(ml_dtypes.bfloat16)


def forward_rows_table():
    cosine, sine = wave(np.arange(N), np.arange(N))
    return np.concatenate([cosine, sine], axis=1).astype(ml_dtypes.bfloat16)


def inverse_rows_table():
    rows = (8 * np.arange(TILES)[None, :] + np.arange(8)[:, None]).reshape(-1)
    cosine, sine = wave(rows, np.arange(N))
    return np.concatenate([cosine, sine], axis=0).astype(ml_dtypes.bfloat16)


def inverse_columns_table():
    cosine, sine = wave(owned_columns(), np.arange(N))
    table = np.stack([2.0 * cosine, -2.0 * sine], axis=1)
    table[0, 0, 0] = 1.0
    table[0, 1, 0] = 1.0 - 2.0 * (np.arange(N) % 2)
    table = table.transpose(2, 0, 1, 3) / N
    return table.reshape(4, 2 * TILES, N).astype(ml_dtypes.bfloat16)


def sum_and_spread_table():
    part, k, patch = np.meshgrid(np.arange(2), np.arange(4), np.arange(4), indexing="ij")
    source = (patch * 8 + part * 4 + k).reshape(-1)
    one = np.repeat(source[:, None] == np.arange(32)[None, :], 8, axis=0)
    return np.tile(one, (1, FRACS)).astype(ml_dtypes.bfloat16)


def dot(a, b, contract):
    return lax.dot_general(a, b, ((contract[:1], contract[1:]), ((), ())), preferred_element_type=F32)


def prepare_kernel(place, groups, filters, pixel, offset, fill_map, weight, flipped, first_rows):
    spot = pixel[...]
    step = offset[...].astype(F32)
    row_key = ((spot >> 7) & 31) * ROWS + (spot >> 12)
    lane_hot = (lax.broadcasted_iota(jnp.int32, (128, spot.shape[1]), 0) == (spot & 127)).astype(F32).astype(BF16)
    for part in range(4):
        rows = lax.broadcasted_iota(jnp.int32, (256, spot.shape[1]), 0) + 256 * part
        row_hot = jnp.where(rows == row_key, step, 0.0).astype(BF16)
        found = dot(row_hot, lane_hot, (1, 1)).astype(BF16)
        for i in range(8):
            lane = (part * 8 + i) * 128
            fill_map[:, lane : lane + 128] = found[i * ROWS : (i + 1) * ROWS]
    square = jnp.zeros(filters.shape[1:], F32)
    for f in range(FRACS):
        square = square + filters[groups[f]] * filters[groups[f]]
    mine = filters[groups[place[0]]] / jnp.sqrt(square)
    turn = (lax.broadcasted_iota(jnp.int32, (N, N), 0) + lax.broadcasted_iota(jnp.int32, (N, N), 1)) & (N - 1)
    turn = (turn == 0).astype(F32).astype(BF16)
    high = mine.astype(BF16)
    low = (mine - high.astype(F32)).astype(BF16)
    back = dot(high, turn, (1, 0)) + dot(low, turn, (1, 0))
    weight[...] = mine
    flipped[...] = back
    first_rows[0:1, :] = mine[0:1]
    first_rows[1:2, :] = back[0:1]


def columns_kernel(frames, gain, above, below, fill_map, table, out, extended, filled):
    for c in range(COLS):
        lanes = slice(c * N, (c + 1) * N)
        extended[8 - RIM : 8, :] = above[:, lanes].astype(F32)
        extended[8 + ROWS : 8 + ROWS + RIM, :] = below[:, lanes].astype(F32)
        value = frames[:, lanes].astype(F32) * gain[:, lanes].astype(F32)
        extended[8 : 8 + ROWS, :] = value
        wanted = fill_map[:, lanes].astype(F32)
        for step in range(-RIM, RIM + 1):
            if step != 0:
                value = jnp.where(wanted == step, extended[8 + step : 8 + step + ROWS, :], value)
        filled[c * ROWS : (c + 1) * ROWS, :] = value.astype(BF16)
    out[...] = dot(table[...], filled[...], (1, 1)).astype(BF16)


def rows_kernel(place, spectrum, weight, flipped, mirror, mirror_first, table, out, by_row, pair):
    tile = place[1]
    lower = tile < TILES // 2
    first = tile == 0
    for k in range(4):
        own = jnp.where(lower, weight[k : k + 1], weight[k + 1 : k + 2])
        if k == 0:
            other = jnp.where(lower, jnp.where(first, flipped[0:1], mirror_first[1:2]), mirror[7:8])
        else:
            other = jnp.where(lower, mirror[8 - k : 9 - k], mirror[7 - k : 8 - k])
        both = 0.5 * (own + other)
        pair[k : k + 1, :] = both
        if k == 0:
            both = jnp.where(first, 0.5 * (mirror_first[0:1] + mirror_first[1:2]), both)
        pair[4 + k : 5 + k, :] = both

    group = lax.broadcasted_iota(jnp.int32, (16, 8, 128), 2) >> 5
    source = spectrum[...].astype(F32).reshape(4, 4, 4, 8, 2 * 128)
    for half in range(2):
        pieces = []
        for j in range(4):
            piece = source[:, :, j, :, half * 128 : (half + 1) * 128].reshape(128, 128)
            pieces.append([piece if d == 0 else pltpu.roll(piece, 32 * d, 1) for d in range(4)])
        for c in range(4):
            found = pieces[3][(3 - c) % 4].reshape(16, 8, 128)
            for j in range(3):
                found = jnp.where(group == j, pieces[j][(j - c) % 4].reshape(16, 8, 128), found)
            for a in range(4):
                for quarter in range(4):
                    by_row[a * 8 + half * 4 + c, :, quarter * 128 : (quarter + 1) * 128] = found[a * 4 + quarter]
    operand = by_row[...].reshape(256, N).astype(BF16)
    scale = pair[...][None]
    with_cosine = dot(operand, table[:, :N], (1, 0)).reshape(32, 8, N) * scale
    with_sine = dot(operand, table[:, N:], (1, 0)).reshape(32, 8, N) * scale
    sign = jnp.where(lax.broadcasted_iota(jnp.int32, (1, 8, 1), 1) < 4, 1.0, -1.0)
    total = with_cosine + sign * pltpu.roll(with_sine, 4, 1)
    out[...] = total.reshape(256, N).astype(BF16)


def back_rows_kernel(parts, spread, table, out, both):
    owned = dot(spread[...], parts[...], (1, 0)).astype(BF16)
    turned = dot(table[...], owned, (1, 1))
    real = turned[:N, :128] - turned[N:, 128:]
    imag = turned[:N, 128:] + turned[N:, :128]
    row = lax.broadcasted_iota(jnp.int32, (TILES, 128), 1) & 7
    for part, value in enumerate((real, imag)):
        picked = value[:TILES]
        for y in range(1, 8):
            picked = jnp.where(row == y, value[y * TILES : (y + 1) * TILES], picked)
        both[pl.ds(part, TILES, stride=2), :] = picked * (1.0 / N)
    out[...] = both[...].astype(BF16)


def back_columns_kernel(spectrum, table, out):
    turned = spectrum[...].astype(F32).T.astype(BF16)
    image = dot(turned[:32], table[0], (1, 0))
    for k in range(1, 4):
        image = image + dot(turned[32 * k : 32 * (k + 1)], table[k], (1, 0))
    out[...] = image.reshape(4, 8, N)


def call(kernel, outs, scratch, scalars, cost, *args):
    smem = pl.BlockSpec(memory_space=pltpu.SMEM)
    vmem = pl.BlockSpec(memory_space=pltpu.VMEM)
    many = isinstance(outs, (list, tuple))
    return pl.pallas_call(
        kernel,
        out_shape=outs,
        in_specs=[smem] * scalars + [vmem] * (len(args) - scalars),
        out_specs=[vmem] * len(outs) if many else vmem,
        scratch_shapes=scratch,
        compiler_params=pltpu.CompilerParams(vmem_limit_bytes=VMEM_LIMIT),
        cost_estimate=pl.CostEstimate(flops=cost, bytes_accessed=1 << 21, transcendentals=0),
    )(*args)


def per_device(frames, gain, defect_pixel, defect_offset, fraction_group, exposure_filter):
    frames = frames.reshape(ROWS, WIDTH)
    place = jnp.stack([lax.axis_index("frac"), lax.axis_index("tile")]).astype(jnp.int32)

    def edge(rows):
        return (frames[rows].astype(F32) * gain[rows].astype(F32)).astype(BF16)

    up = [(i, i + 1) for i in range(TILES - 1)]
    above = lax.ppermute(edge(slice(ROWS - RIM, ROWS)), "tile", up)
    below = lax.ppermute(edge(slice(0, RIM)), "tile", [(b, a) for a, b in up])

    shape = jax.ShapeDtypeStruct
    fill_map, weight, flipped, first_rows = call(
        prepare_kernel,
        [shape((ROWS, WIDTH), BF16), shape((8, N), F32), shape((8, N), F32), shape((2, N), F32)],
        [],
        2,
        1 << 27,
        place,
        fraction_group,
        exposure_filter,
        defect_pixel.reshape(1, -1),
        defect_offset.reshape(1, -1),
    )
    half = TILES // 2
    mirror = lax.ppermute(flipped, "tile", [(t, TILES - 1 - t) for t in range(TILES)])
    mirror_first = lax.ppermute(
        first_rows, "tile", [(half, 0)] + [(t, TILES - t) for t in range(half + 1, TILES)]
    )

    columns = call(
        columns_kernel,
        shape((N, COLS * ROWS), BF16),
        [pltpu.VMEM((ROWS + 16, N), F32), pltpu.VMEM((COLS * ROWS, N), BF16)],
        0,
        1 << 27,
        frames,
        gain,
        above,
        below,
        fill_map,
        jnp.asarray(forward_columns_table()),
    )
    columns = lax.all_to_all(columns.reshape(TILES, 8, COLS * ROWS), "tile", 0, 0, tiled=True)

    weighted = call(
        rows_kernel,
        shape((256, N), BF16),
        [pltpu.VMEM((32, 8, N), F32), pltpu.VMEM((8, N), F32)],
        1,
        1 << 28,
        place,
        columns.reshape(N, COLS * ROWS),
        weight,
        flipped,
        mirror,
        mirror_first,
        jnp.asarray(forward_rows_table()),
    )
    parts = lax.all_to_all(weighted.reshape(FRACS, 32, N), "frac", 0, 0, tiled=True)

    back = call(
        back_rows_kernel,
        shape((2 * TILES, 128), BF16),
        [pltpu.VMEM((2 * TILES, 128), F32)],
        0,
        1 << 28,
        parts.reshape(256, N),
        jnp.asarray(sum_and_spread_table()),
        jnp.asarray(inverse_rows_table()),
    )
    back = lax.all_to_all(back.reshape(TILES, 2, 128), "tile", 0, 0, tiled=True)

    return call(
        back_columns_kernel,
        shape((4, 8, N), F32),
        [],
        0,
        1 << 26,
        back.reshape(2 * TILES, 128),
        jnp.asarray(inverse_columns_table()),
    )


def solution(mesh):
    return jax.shard_map(
        per_device,
        mesh=mesh,
        in_specs=(
            P("frac", "tile", None),
            P("tile", None),
            P("tile"),
            P("tile"),
            P(),
            P(None, "tile", None),
        ),
        out_specs=P("frac", "tile", None),
        check_vma=False,
    )
```

profile of v0, /device:TPU:2, one launch (start us, length us, event | category | flops | bytes accessed | tf_op | source)
XLA Modules:
  0.0 95.1 jit_solution(10036420091095110226)
XLA Ops:
  0.0 0.0 copy-start.2
  0.0 1.0 %fusion = (bf16[4,4096]{1,0:T(4,128)(2,1)S(1)}, bf16[4,4096]{1,0:T(4,128)(2,1)S(1)}) fusion(bf16[32,4096]{1,0:T(8,128)(2,1)} %gain.1, bf16[1,32,4096]{2,1,0:T(8,128)(2,1)} %param.11), kind=kLoop, calls=%fused_computation.1 | loop fusion | flops 131072 | bytes 196608 | tf_op jit(solution)/shard_map/convert_element_type | solution.py:193
  1.1 11.4 %collective-permute-start.1 = (bf16[4,4096]{1,0:T(4,128)(2,1)S(1)}, bf16[4,4096]{1,0:T(4,128)(2,1)S(1)}, u32[]{:S(2)}, u32[]{:S(2)}) collective-permute-start(bf16[4,4096]{1,0:T(4,128)(2,1)S(1)} %get-tuple-element.13), channel_id=1, source_target_pairs={{1,0},{2,1},{3,2},{4,3},{5,4},{6,5},{7,6},{8,7},{9,8},{10,9},{11,1... | collective-permute-start | bytes 98312 | tf_op jit(solution)/shard_map/ppermute | solution.py:197
  12.4 1.9 %collective-permute-start = (bf16[4,4096]{1,0:T(4,128)(2,1)S(1)}, bf16[4,4096]{1,0:T(4,128)(2,1)S(1)}, u32[]{:S(2)}, u32[]{:S(2)}) collective-permute-start(bf16[4,4096]{1,0:T(4,128)(2,1)S(1)} %get-tuple-element.14), channel_id=1, source_target_pairs={{0,1},{1,2},{2,3},{3,4},{4,5},{5,6},{6,7},{7,8},{8,9},{9,10},{10,1... | collective-permute-start | bytes 98312 | tf_op jit(solution)/shard_map/ppermute | solution.py:196
  14.4 0.1 pad_add_fusion.place
  14.4 0.0 copy-start.7
  14.4 0.9 copy-done.7
  15.3 0.0 copy-start.8
  15.3 0.7 copy-done.8
  16.0 0.0 copy-start.9
  16.0 0.7 copy-done.9
  16.7 0.0 copy-start.10
  16.7 0.7 copy-done.10
  17.4 1.1 %shard_map.109 = (bf16[32,4096]{1,0:T(8,128)(2,1)S(1)}, f32[8,512]{1,0:T(8,128)S(1)}, f32[8,512]{1,0:T(8,128)S(1)}, f32[2,512]{1,0:T(2,128)S(1)}) custom-call(s32[2]{0:T(128)S(1)} %pad_add_fusion.place, s32[8]{0:T(128)S(1)} %copy-done.10, f32[8,8,512]{2,1,0:T(8,128)S(1)} %copy-done.7, s32[1,512]{1,0:T(1,128)S(1)} %bitcast.23, s32[1,512]{1,0:T(1,128)S(1)} %bitcast.24), custom_call_target="tpu_custom_call" | custom-call | flops 134217728 | bytes 2097152 | tf_op jit(solution)/shard_map/pallas_call | solution.py:177
  18.4 0.0 collective-permute-done.1.below
  18.4 1.9 %collective-permute-done.above = bf16[4,4096]{1,0:T(4,128)(2,1)S(1)} collective-permute-done((bf16[4,4096]{1,0:T(4,128)(2,1)S(1)}, bf16[4,4096]{1,0:T(4,128)(2,1)S(1)}, u32[]{:S(2)}, u32[]{:S(2)}) %collective-permute-start) | collective-permute-done | bytes 32800 | tf_op jit(solution)/shard_map/ppermute | solution.py:196
  20.4 0.0 copy-done.2
  20.4 0.0 copy-start.4
  20.4 0.9 copy-done.4
  21.3 0.0 copy-start.5
  21.3 0.9 copy-done.5
  22.3 0.0 copy-start
  22.3 1.8 %shard_map.110 = bf16[512,256]{1,0:T(8,128)(2,1)} custom-call(bf16[32,4096]{1,0:T(8,128)(2,1)S(1)} %bitcast.20, bf16[32,4096]{1,0:T(8,128)(2,1)S(1)} %copy-done.5, bf16[4,4096]{1,0:T(4,128)(2,1)S(1)} %collective-permute-done.above, bf16[4,4096]{1,0:T(4,128)(2,1)S(1)} %collective-permute-done.1.below, bf16[32,4096]{1,0:T(8,128)(2,1)S(1)} %get-tuple-element.9.fill_map, ...), custom_call_target="tpu_custom_call" | custom-call | flops 134217728 | bytes 2097152 | tf_op jit(solution)/shard_map/pallas_call | solution.py:177
  24.0 9.3 %all-to-all-start = ((bf16[64,8,256]{2,1,0:T(8,128)(2,1)}), bf16[64,8,256]{2,1,0:T(8,128)(2,1)S(1)}, u32[]{:S(2)}, u32[]{:S(2)}) async-start(bf16[64,8,256]{2,1,0:T(8,128)(2,1)} %bitcast.7), calls=%async_computation | async-start | bytes 524288 | tf_op jit(solution)/shard_map/all_to_all | solution.py:231
  33.3 5.7 %collective-permute-start.2 = (f32[8,512]{1,0:T(8,128)S(1)}, f32[8,512]{1,0:T(8,128)S(1)}, u32[]{:S(2)}, u32[]{:S(2)}) collective-permute-start(f32[8,512]{1,0:T(8,128)S(1)} %get-tuple-element.11.flipped), channel_id=1, source_target_pairs={{0,63},{1,62},{2,61},{3,60},{4,59},{5,58},{6,57},{7,56},{8,55},{9,... | collective-permute-start | bytes 49160 | tf_op jit(solution)/shard_map/ppermute | solution.py:213
  39.0 1.3 %collective-permute-start.3 = (f32[2,512]{1,0:T(2,128)S(1)}, f32[2,512]{1,0:T(2,128)S(1)}, u32[]{:S(2)}, u32[]{:S(2)}) collective-permute-start(f32[2,512]{1,0:T(2,128)S(1)} %get-tuple-element.12), channel_id=1, source_target_pairs={{32,0},{33,31},{34,30},{35,29},{36,28},{37,27},{38,26},{39,25},{40... | collective-permute-start | bytes 12296 | tf_op jit(solution)/shard_map/ppermute | solution.py:214
  40.3 5.7 %collective-permute-done.3.mirror_first = f32[2,512]{1,0:T(2,128)S(1)} collective-permute-done((f32[2,512]{1,0:T(2,128)S(1)}, f32[2,512]{1,0:T(2,128)S(1)}, u32[]{:S(2)}, u32[]{:S(2)}) %collective-permute-start.3) | collective-permute-done | bytes 4128 | tf_op jit(solution)/shard_map/ppermute | solution.py:214
  46.0 1.9 %collective-permute-done.2.mirror = f32[8,512]{1,0:T(8,128)S(1)} collective-permute-done((f32[8,512]{1,0:T(8,128)S(1)}, f32[8,512]{1,0:T(8,128)S(1)}, u32[]{:S(2)}, u32[]{:S(2)}) %collective-permute-start.2) | collective-permute-done | bytes 16416 | tf_op jit(solution)/shard_map/ppermute | solution.py:213
  47.9 5.2 %all-to-all-done = bf16[64,8,256]{2,1,0:T(8,128)(2,1)S(1)} async-done(((bf16[64,8,256]{2,1,0:T(8,128)(2,1)}), bf16[64,8,256]{2,1,0:T(8,128)(2,1)S(1)}, u32[]{:S(2)}, u32[]{:S(2)}) %all-to-all-start) | async-done | bytes 262176 | tf_op jit(solution)/shard_map/all_to_all | solution.py:231
  53.1 0.0 copy-done
  53.1 0.0 copy-start.1
  53.1 1.1 %shard_map.111 = bf16[256,512]{1,0:T(8,128)(2,1)S(1)} custom-call(s32[2]{0:T(128)S(1)} %pad_add_fusion.place, bf16[512,256]{1,0:T(8,128)(2,1)S(1)} %bitcast.17, f32[8,512]{1,0:T(8,128)S(1)} %get-tuple-element.10.weight, f32[8,512]{1,0:T(8,128)S(1)} %get-tuple-element.11.flipped, f32[8,512]{1,0:T(8,128)S(1)} %collective-permute-done.2.mirror, ...), custom_call_target="tpu_custom_call" | custom-call | flops 268435456 | bytes 2097152 | tf_op jit(solution)/shard_map/pallas_call | solution.py:177
  54.2 0.0 copy-start.6
  54.2 11.9 %all_to_all.15 = bf16[8,32,512]{2,1,0:T(8,128)(2,1)S(1)} all-to-all(bf16[8,32,512]{2,1,0:T(8,128)(2,1)S(1)} %bitcast.18), channel_id=1, replica_groups=mesh['frac'=8,'tile'=64] {'frac'}, dimensions={0} | all-to-all | bytes 524288 | tf_op jit(solution)/shard_map/all_to_all | solution.py:247
  66.2 0.0 copy-done.1
  66.2 0.0 copy-done.6
  66.2 0.0 copy-start.3
  66.2 0.6 shard_map.112
  66.8 27.4 %all_to_all.16 = bf16[64,2,128]{2,1,0:T(2,128)(2,1)S(1)} all-to-all(bf16[64,2,128]{2,1,0:T(2,128)(2,1)S(1)} %bitcast.21), channel_id=1, replica_groups=mesh['frac'=8,'tile'=64] {'tile'}, dimensions={0} | all-to-all | bytes 65536 | tf_op jit(solution)/shard_map/all_to_all | solution.py:259
  94.2 0.0 copy-done.3
  94.2 0.9 shard_map.113
Async XLA Ops:
  0.0 20.4 %copy-start.2 = (bf16[512,512]{1,0:T(8,128)(2,1)S(1)}, bf16[512,512]{1,0:T(8,128)(2,1)}, u32[]{:S(2)}) copy-start(bf16[512,512]{1,0:T(8,128)(2,1)} %constant.19.clone.table) | copy-start | bytes 1572868
  1.1 17.4 %collective-permute-start.1 = (bf16[4,4096]{1,0:T(4,128)(2,1)S(1)}, bf16[4,4096]{1,0:T(4,128)(2,1)S(1)}, u32[]{:S(2)}, u32[]{:S(2)}) collective-permute-start(bf16[4,4096]{1,0:T(4,128)(2,1)S(1)} %get-tuple-element.13), channel_id=1, source_target_pairs={{1,0},{2,1},{3,2},{4,3},{5,4},{6,5},{7,6},{8,7},{9,8},{10,9},{11,1... | collective-permute-start | bytes 98312 | tf_op jit(solution)/shard_map/ppermute | solution.py:197
  12.4 7.9 %collective-permute-start = (bf16[4,4096]{1,0:T(4,128)(2,1)S(1)}, bf16[4,4096]{1,0:T(4,128)(2,1)S(1)}, u32[]{:S(2)}, u32[]{:S(2)}) collective-permute-start(bf16[4,4096]{1,0:T(4,128)(2,1)S(1)} %get-tuple-element.14), channel_id=1, source_target_pairs={{0,1},{1,2},{2,3},{3,4},{4,5},{5,6},{6,7},{7,8},{8,9},{9,10},{10,1... | collective-permute-start | bytes 98312 | tf_op jit(solution)/shard_map/ppermute | solution.py:196
  14.4 0.9 copy-start.7
  15.3 0.7 copy-start.8
  16.0 0.7 copy-start.9
  16.7 0.7 copy-start.10
  20.4 1.0 %copy-start.4 = (bf16[1,32,4096]{2,1,0:T(8,128)(2,1)S(1)}, bf16[1,32,4096]{2,1,0:T(8,128)(2,1)}, u32[]{:S(2)}) copy-start(bf16[1,32,4096]{2,1,0:T(8,128)(2,1)} %param.11) | copy-start | bytes 786436
  21.3 0.9 copy-start.5
  22.3 30.9 %copy-start = (bf16[512,1024]{1,0:T(8,128)(2,1)S(1)}, bf16[512,1024]{1,0:T(8,128)(2,1)}, u32[]{:S(2)}) copy-start(bf16[512,1024]{1,0:T(8,128)(2,1)} %constant.20.clone.table) | copy-start | bytes 3145732
  24.0 29.1 %all-to-all-start = ((bf16[64,8,256]{2,1,0:T(8,128)(2,1)}), bf16[64,8,256]{2,1,0:T(8,128)(2,1)S(1)}, u32[]{:S(2)}, u32[]{:S(2)}) async-start(bf16[64,8,256]{2,1,0:T(8,128)(2,1)} %bitcast.7), calls=%async_computation | async-start | bytes 524288 | tf_op jit(solution)/shard_map/all_to_all | solution.py:231
  33.3 14.6 %collective-permute-start.2 = (f32[8,512]{1,0:T(8,128)S(1)}, f32[8,512]{1,0:T(8,128)S(1)}, u32[]{:S(2)}, u32[]{:S(2)}) collective-permute-start(f32[8,512]{1,0:T(8,128)S(1)} %get-tuple-element.11.flipped), channel_id=1, source_target_pairs={{0,63},{1,62},{2,61},{3,60},{4,59},{5,58},{6,57},{7,56},{8,55},{9,... | collective-permute-start | bytes 49160 | tf_op jit(solution)/shard_map/ppermute | solution.py:213
  39.0 7.0 %collective-permute-start.3 = (f32[2,512]{1,0:T(2,128)S(1)}, f32[2,512]{1,0:T(2,128)S(1)}, u32[]{:S(2)}, u32[]{:S(2)}) collective-permute-start(f32[2,512]{1,0:T(2,128)S(1)} %get-tuple-element.12), channel_id=1, source_target_pairs={{32,0},{33,31},{34,30},{35,29},{36,28},{37,27},{38,26},{39,25},{40... | collective-permute-start | bytes 12296 | tf_op jit(solution)/shard_map/ppermute | solution.py:214
  53.1 13.1 %copy-start.1 = (bf16[1024,512]{1,0:T(8,128)(2,1)S(1)}, bf16[1024,512]{1,0:T(8,128)(2,1)}, u32[]{:S(2)}) copy-start(bf16[1024,512]{1,0:T(8,128)(2,1)} %constant.22.clone.table) | copy-start | bytes 3145732
  54.2 12.0 %copy-start.6 = (bf16[256,256]{1,0:T(8,128)(2,1)S(1)}, bf16[256,256]{1,0:T(8,128)(2,1)}, u32[]{:S(2)}) copy-start(bf16[256,256]{1,0:T(8,128)(2,1)} %constant.21.clone.spread) | copy-start | bytes 393220
  66.2 28.0 %copy-start.3 = (bf16[4,128,512]{2,1,0:T(8,128)(2,1)S(1)}, bf16[4,128,512]{2,1,0:T(8,128)(2,1)}, u32[]{:S(2)}) copy-start(bf16[4,128,512]{2,1,0:T(8,128)(2,1)} %constant.23.clone.table) | copy-start | bytes 1572868
where the time goes:
time: 95.6 us; the launch traced here: 95.1 us
  blocking collectives  39.3 us (41%)
  starting transfers between devices  29.6 us (31%)
  waiting for transfers between devices  14.7 us (15%)
  Pallas kernels  5.44 us (6%)
  local copies, waits for them, and re-layouts  4.84 us (5%)
  other arithmetic  1.12 us (1%)
    all_to_all x1, blocking collectives, per_device(): back = lax.all_to_all(back.reshape(TILES, 2, 128), 'tile', 0, 0, tiled=True)  27.4 us
    all_to_all x1, blocking collectives, per_device(): lax.all_to_all(weighted.reshape(FRACS, 32, N), 'frac', 0, 0, tiled=True)  11.9 us
    ppermute x1, starting transfers between devices, per_device(): below = lax.ppermute(edge(slice(0, RIM)), 'tile', [(b, a) for a, b in up])  11.4 us
    all_to_all x1, starting transfers between devices, per_device(): lax.all_to_all(columns.reshape(TILES, 8, COLS * ROWS), 'tile', 0, 0, tile...  9.3 us
    ppermute x1, waiting for transfers between devices, per_device(): lax.ppermute(first_rows, 'tile', [(half, 0)] + [(t, TILES - t) for t in r...  5.71 us
    ppermute x1, starting transfers between devices, per_device(): lax.ppermute(flipped, 'tile', [(t, TILES - 1 - t) for t in range(TILES)])  5.68 us
    pallas_call x5, Pallas kernels, call(): pl.pallas_call(kernel, out_shape=outs, in_specs=[smem] * scalars + [vmem]...  5.44 us
    all_to_all x1, waiting for transfers between devices, per_device(): lax.all_to_all(columns.reshape(TILES, 8, COLS * ROWS), 'tile', 0, 0, tile...  5.22 us
  transfers between devices with their start and end apart: 5, of which 4 were waited for; matrix products, arithmetic and copies ran while one was open for 0% of the time, Pallas kernels for 1%

commit v1 on v0

--- a/solution.py
+++ b/solution.py
@@ -10,6 +10,7 @@
 N = 512
 RIM = 4
 TILES = 64
+HALF = TILES // 2
 FRACS = 8
 COLS = 8
 ROWS = 32
@@ -26,13 +27,14 @@
 
 def owned_columns():
     tile = np.arange(TILES)[:, None]
-    return 8 * tile + np.arange(4)[None, :] + (tile >= TILES // 2)
+    near = np.array([1, 2, 3, 4])[None, :]
+    return 8 * tile + np.where(tile < HALF, np.array([1, 2, 3, 8])[None, :], near)
 
 
 def forward_columns_table():
     cosine, sine = wave(owned_columns(), np.arange(N))
     table = np.stack([cosine, -sine], axis=1)
-    table[0, 1, 0] = 1.0 - 2.0 * (np.arange(N) % 2)
+    table[HALF - 1, 1, 3] = 1.0
     return table.reshape(N, N).astype(ml_dtypes.bfloat16)
 
 
@@ -50,8 +52,8 @@
 def inverse_columns_table():
     cosine, sine = wave(owned_columns(), np.arange(N))
     table = np.stack([2.0 * cosine, -2.0 * sine], axis=1)
-    table[0, 0, 0] = 1.0
-    table[0, 1, 0] = 1.0 - 2.0 * (np.arange(N) % 2)
+    table[HALF - 1, 0, 3] = 1.0 - 2.0 * (np.arange(N) % 2)
+    table[HALF - 1, 1, 3] = 1.0
     table = table.transpose(2, 0, 1, 3) / N
     return table.reshape(4, 2 * TILES, N).astype(ml_dtypes.bfloat16)
 
@@ -67,18 +69,7 @@
     return lax.dot_general(a, b, ((contract[:1], contract[1:]), ((), ())), preferred_element_type=F32)
 
 
-def prepare_kernel(place, groups, filters, pixel, offset, fill_map, weight, flipped, first_rows):
-    spot = pixel[...]
-    step = offset[...].astype(F32)
-    row_key = ((spot >> 7) & 31) * ROWS + (spot >> 12)
-    lane_hot = (lax.broadcasted_iota(jnp.int32, (128, spot.shape[1]), 0) == (spot & 127)).astype(F32).astype(BF16)
-    for part in range(4):
-        rows = lax.broadcasted_iota(jnp.int32, (256, spot.shape[1]), 0) + 256 * part
-        row_hot = jnp.where(rows == row_key, step, 0.0).astype(BF16)
-        found = dot(row_hot, lane_hot, (1, 1)).astype(BF16)
-        for i in range(8):
-            lane = (part * 8 + i) * 128
-            fill_map[:, lane : lane + 128] = found[i * ROWS : (i + 1) * ROWS]
+def weights_kernel(place, groups, filters, weight, mirror, first_rows):
     square = jnp.zeros(filters.shape[1:], F32)
     for f in range(FRACS):
         square = square + filters[groups[f]] * filters[groups[f]]
@@ -89,40 +80,82 @@
     low = (mine - high.astype(F32)).astype(BF16)
     back = dot(high, turn, (1, 0)) + dot(low, turn, (1, 0))
     weight[...] = mine
-    flipped[...] = back
+    mirror[...] = back
+    mirror[0:1, :] = mine[0:1]
+    mirror[1:2, :] = back[0:1]
     first_rows[0:1, :] = mine[0:1]
     first_rows[1:2, :] = back[0:1]
 
 
-def columns_kernel(frames, gain, above, below, fill_map, table, out, extended, filled):
+def fill_kernel(pixel_in, offset_in, frames_in, gain_in, filled, edges, pixel, offset, frames, gain, fill_map, extended, sems):
+    pairs = ((pixel_in, pixel), (offset_in, offset), (frames_in, frames), (gain_in, gain))
+    copies = [pltpu.make_async_copy(a, b, sems.at[i]) for i, (a, b) in enumerate(pairs)]
+    for copy in copies:
+        copy.start()
+    copies[0].wait()
+    copies[1].wait()
+    spot = pixel[...]
+    step = offset[...].astype(F32)
+    row_key = ((spot >> 7) & 31) * ROWS + (spot >> 12)
+    lane_hot = (lax.broadcasted_iota(jnp.int32, (128, spot.shape[1]), 0) == (spot & 127)).astype(F32).astype(BF16)
+    for part in range(4):
+        rows = lax.broadcasted_iota(jnp.int32, (256, spot.shape[1]), 0) + 256 * part
+        row_hot = jnp.where(rows == row_key, step, 0.0).astype(BF16)
+        found = dot(row_hot, lane_hot, (1, 1))
+        for i in range(8):
+            lane = (part * 8 + i) * 128
+            fill_map[:, lane : lane + 128] = found[i * ROWS : (i + 1) * ROWS]
+    copies[2].wait()
+    copies[3].wait()
+    extended[0:8, :] = jnp.zeros((8, N), F32)
+    extended[8 + ROWS : 16 + ROWS, :] = jnp.zeros((8, N), F32)
     for c in range(COLS):
         lanes = slice(c * N, (c + 1) * N)
-        extended[8 - RIM : 8, :] = above[:, lanes].astype(F32)
-        extended[8 + ROWS : 8 + ROWS + RIM, :] = below[:, lanes].astype(F32)
         value = frames[:, lanes].astype(F32) * gain[:, lanes].astype(F32)
         extended[8 : 8 + ROWS, :] = value
-        wanted = fill_map[:, lanes].astype(F32)
+        wanted = fill_map[:, lanes]
+        edges[0:8, lanes] = wanted[0:8]
+        edges[8:16, lanes] = wanted[ROWS - 8 : ROWS]
         for step in range(-RIM, RIM + 1):
             if step != 0:
                 value = jnp.where(wanted == step, extended[8 + step : 8 + step + ROWS, :], value)
         filled[c * ROWS : (c + 1) * ROWS, :] = value.astype(BF16)
-    out[...] = dot(table[...], filled[...], (1, 1)).astype(BF16)
-
-
-def rows_kernel(place, spectrum, weight, flipped, mirror, mirror_first, table, out, by_row, pair):
+
+
+def columns_kernel(above, below, filled, edges, table, out, halo, operand):
+    halo[...] = jnp.zeros(halo.shape, F32)
+    halo[4:8, :] = above[...].astype(F32)
+    halo[24:28, :] = below[...].astype(F32)
+    for c in range(COLS):
+        lanes = slice(c * N, (c + 1) * N)
+        top = jnp.zeros((8, N), F32)
+        bottom = jnp.zeros((8, N), F32)
+        for step in range(1, RIM + 1):
+            top = top + jnp.where(edges[0:8, lanes] == -step, halo[8 - step : 16 - step, lanes], 0.0)
+            bottom = bottom + jnp.where(edges[8:16, lanes] == step, halo[16 + step : 24 + step, lanes], 0.0)
+        rows = filled[c * ROWS : (c + 1) * ROWS, :].astype(F32)
+        rows = jnp.concatenate([rows[0:8] + top, rows[8 : ROWS - 8], rows[ROWS - 8 :] + bottom], axis=0)
+        operand[c * ROWS : (c + 1) * ROWS, :] = rows.astype(BF16)
+    out[...] = dot(table[...], operand[...], (1, 1)).astype(BF16)
+
+
+def rows_kernel(place, spectrum, weight, mirror, following, table, out, by_row, pair):
     tile = place[1]
-    lower = tile < TILES // 2
-    first = tile == 0
+    lower = tile < HALF
+    last = tile == HALF - 1
     for k in range(4):
-        own = jnp.where(lower, weight[k : k + 1], weight[k + 1 : k + 2])
-        if k == 0:
-            other = jnp.where(lower, jnp.where(first, flipped[0:1], mirror_first[1:2]), mirror[7:8])
+        if k < 3:
+            own = weight[k + 1 : k + 2]
+            other = mirror[7 - k : 8 - k]
         else:
-            other = jnp.where(lower, mirror[8 - k : 9 - k], mirror[7 - k : 8 - k])
+            own = jnp.where(lower, following[0:1], weight[4:5])
+            other = jnp.where(lower, mirror[1:2], mirror[4:5])
         both = 0.5 * (own + other)
-        pair[k : k + 1, :] = both
-        if k == 0:
-            both = jnp.where(first, 0.5 * (mirror_first[0:1] + mirror_first[1:2]), both)
+        if k == 3:
+            pair[3:4, :] = jnp.where(last, 0.5 * (mirror[0:1] + mirror[1:2]), both)
+            both = jnp.where(last, 0.5 * (following[0:1] + following[1:2]), both)
+        else:
+            pair[k : k + 1, :] = both
         pair[4 + k : 5 + k, :] = both
 
     group = lax.broadcasted_iota(jnp.int32, (16, 8, 128), 2) >> 5
@@ -170,14 +203,14 @@
     out[...] = image.reshape(4, 8, N)
 
 
-def call(kernel, outs, scratch, scalars, cost, *args):
+def call(kernel, outs, scratch, scalars, cost, *args, space=pltpu.VMEM):
     smem = pl.BlockSpec(memory_space=pltpu.SMEM)
     vmem = pl.BlockSpec(memory_space=pltpu.VMEM)
     many = isinstance(outs, (list, tuple))
     return pl.pallas_call(
         kernel,
         out_shape=outs,
-        in_specs=[smem] * scalars + [vmem] * (len(args) - scalars),
+        in_specs=[smem] * scalars + [pl.BlockSpec(memory_space=space)] * (len(args) - scalars),
         out_specs=[vmem] * len(outs) if many else vmem,
         scratch_shapes=scratch,
         compiler_params=pltpu.CompilerParams(vmem_limit_bytes=VMEM_LIMIT),
@@ -197,35 +230,50 @@
     below = lax.ppermute(edge(slice(0, RIM)), "tile", [(b, a) for a, b in up])
 
     shape = jax.ShapeDtypeStruct
-    fill_map, weight, flipped, first_rows = call(
-        prepare_kernel,
-        [shape((ROWS, WIDTH), BF16), shape((8, N), F32), shape((8, N), F32), shape((2, N), F32)],
+    weight, mirror, first_rows = call(
+        weights_kernel,
+        [shape((8, N), F32), shape((8, N), F32), shape((2, N), F32)],
         [],
         2,
-        1 << 27,
+        1 << 23,
         place,
         fraction_group,
         exposure_filter,
+    )
+    mirror = lax.ppermute(mirror, "tile", [(t, TILES - 1 - t) for t in range(TILES)])
+    following = lax.ppermute(first_rows, "tile", [((t + 1) % HALF, t) for t in range(HALF)])
+
+    defects = defect_pixel.shape[0]
+    filled, edges = call(
+        fill_kernel,
+        [shape((COLS * ROWS, N), BF16), shape((16, WIDTH), F32)],
+        [
+            pltpu.VMEM((1, defects), jnp.int32),
+            pltpu.VMEM((1, defects), jnp.int32),
+            pltpu.VMEM((ROWS, WIDTH), BF16),
+            pltpu.VMEM((ROWS, WIDTH), BF16),
+            pltpu.VMEM((ROWS, WIDTH), F32),
+            pltpu.VMEM((ROWS + 16, N), F32),
+            pltpu.SemaphoreType.DMA((4,)),
+        ],
+        0,
+        1 << 27,
         defect_pixel.reshape(1, -1),
         defect_offset.reshape(1, -1),
-    )
-    half = TILES // 2
-    mirror = lax.ppermute(flipped, "tile", [(t, TILES - 1 - t) for t in range(TILES)])
-    mirror_first = lax.ppermute(
-        first_rows, "tile", [(half, 0)] + [(t, TILES - t) for t in range(half + 1, TILES)]
-    )
-
+        frames,
+        gain,
+        space=pltpu.HBM,
+    )
     columns = call(
         columns_kernel,
         shape((N, COLS * ROWS), BF16),
-        [pltpu.VMEM((ROWS + 16, N), F32), pltpu.VMEM((COLS * ROWS, N), BF16)],
+        [pltpu.VMEM((32, WIDTH), F32), pltpu.VMEM((COLS * ROWS, N), BF16)],
         0,
         1 << 27,
-        frames,
-        gain,
         above,
         below,
-        fill_map,
+        filled,
+        edges,
         jnp.asarray(forward_columns_table()),
     )
     columns = lax.all_to_all(columns.reshape(TILES, 8, COLS * ROWS), "tile", 0, 0, tiled=True)
@@ -239,9 +287,8 @@
         place,
         columns.reshape(N, COLS * ROWS),
         weight,
-        flipped,
         mirror,
-        mirror_first,
+        following,
         jnp.asarray(forward_rows_table()),
     )
     parts = lax.all_to_all(weighted.reshape(FRACS, 32, N), "frac", 0, 0, tiled=True)

time: 95.6 us -> 89.4 us (0.935)
  waiting for transfers between devices: 14.7 us -> 8.97 us
  starting transfers between devices: 29.6 us -> 35.2 us
  blocking collectives: 39.3 us -> 33.7 us
  local copies, waits for them, and re-layouts: 4.84 us -> 3.86 us
    all_to_all x1, blocking collectives: 27.4 us -> 21.8 us  [per_device(): back = lax.all_to_all(back.reshape(TILES, 2, 128), 'tile', 0, 0, tiled=True)]
    ppermute x2, waiting for transfers between devices: 7.57 us -> 3.64 us  [the longest x1 2.54 us: per_device(): lax.ppermute(first_rows, 'tile', [((t + 1) % HALF, t) for t in range(HALF)])]
    all_to_all x1, starting transfers between devices: 9.3 us -> 12.5 us  [per_device(): lax.all_to_all(columns.reshape(TILES, 8, COLS * ROWS), 'tile', 0, 0, tile...]
    ppermute x2, starting transfers between devices: 6.97 us -> 9.36 us  [the longest x1 5.67 us: per_device(): lax.ppermute(mirror, 'tile', [(t, TILES - 1 - t) for t in range(TILES)])]
    ppermute x1, waiting for transfers between devices: 1.92 us -> 0.01 us  [per_device(): above = lax.ppermute(edge(slice(ROWS - RIM, ROWS)), 'tile', up)]
    ppermute x1, starting transfers between devices: 11.4 us -> 9.47 us  [per_device(): below = lax.ppermute(edge(slice(0, RIM)), 'tile', [(b, a) for a, b in up])]
    ppermute x1, starting transfers between devices: 1.92 us -> 3.83 us  [per_device(): above = lax.ppermute(edge(slice(ROWS - RIM, ROWS)), 'tile', up)]
    unnamed x22, local copies, waits for them, and re-layouts: 4.84 us -> 3.86 us
  transfers between devices with their start and end apart: 5 -> 5, of which waited for: 4 -> 3; matrix products, arithmetic and copies ran while one was open for 0% -> 0% of each run, Pallas kernels for 1% -> 2%
where the time goes in v1:
time: 89.4 us; the launch traced here: 88.9 us
  starting transfers between devices  35.2 us (39%)
  blocking collectives  33.7 us (38%)
  waiting for transfers between devices  8.97 us (10%)
  Pallas kernels  5.93 us (7%)
  local copies, waits for them, and re-layouts  3.86 us (4%)
  other arithmetic  1.12 us (1%)
    all_to_all x1, blocking collectives, per_device(): back = lax.all_to_all(back.reshape(TILES, 2, 128), 'tile', 0, 0, tiled=True)  21.8 us
    all_to_all x1, starting transfers between devices, per_device(): lax.all_to_all(columns.reshape(TILES, 8, COLS * ROWS), 'tile', 0, 0, tile...  12.5 us
    all_to_all x1, blocking collectives, per_device(): lax.all_to_all(weighted.reshape(FRACS, 32, N), 'frac', 0, 0, tiled=True)  11.9 us
    ppermute x1, starting transfers between devices, per_device(): below = lax.ppermute(edge(slice(0, RIM)), 'tile', [(b, a) for a, b in up])  9.47 us
    pallas_call x6, Pallas kernels, call(): pl.pallas_call(kernel, out_shape=outs, in_specs=[smem] * scalars + [pl.Bl...  5.93 us
    ppermute x1, starting transfers between devices, per_device(): lax.ppermute(mirror, 'tile', [(t, TILES - 1 - t) for t in range(TILES)])  5.67 us
    all_to_all x1, waiting for transfers between devices, per_device(): lax.all_to_all(columns.reshape(TILES, 8, COLS * ROWS), 'tile', 0, 0, tile...  5.33 us
    unnamed x22, local copies, waits for them, and re-layouts  3.86 us
  transfers between devices with their start and end apart: 5, of which 3 were waited for; matrix products, arithmetic and copies ran while one was open for 0% of the time, Pallas kernels for 2%

profile of v1, /device:TPU:2, one launch (start us, length us, event | category | flops | bytes accessed | tf_op | source)
XLA Modules:
  0.0 88.9 jit_solution(3313907506650395649)
XLA Ops:
  0.0 0.0 copy-start.3
  0.0 1.0 %fusion = (bf16[4,4096]{1,0:T(4,128)(2,1)S(1)}, bf16[4,4096]{1,0:T(4,128)(2,1)S(1)}) fusion(bf16[32,4096]{1,0:T(8,128)(2,1)} %gain_in.1, bf16[1,32,4096]{2,1,0:T(8,128)(2,1)} %param.11), kind=kLoop, calls=%fused_computation.1 | loop fusion | flops 131072 | bytes 196608 | tf_op jit(solution)/shard_map/convert_element_type | solution.py:226
  1.1 3.8 %collective-permute-start = (bf16[4,4096]{1,0:T(4,128)(2,1)S(1)}, bf16[4,4096]{1,0:T(4,128)(2,1)S(1)}, u32[]{:S(2)}, u32[]{:S(2)}) collective-permute-start(bf16[4,4096]{1,0:T(4,128)(2,1)S(1)} %get-tuple-element.16), channel_id=1, source_target_pairs={{0,1},{1,2},{2,3},{3,4},{4,5},{5,6},{6,7},{7,8},{8,9},{9,10},{10,1... | collective-permute-start | bytes 98312 | tf_op jit(solution)/shard_map/ppermute | solution.py:229
  4.9 9.5 %collective-permute-start.1 = (bf16[4,4096]{1,0:T(4,128)(2,1)S(1)}, bf16[4,4096]{1,0:T(4,128)(2,1)S(1)}, u32[]{:S(2)}, u32[]{:S(2)}) collective-permute-start(bf16[4,4096]{1,0:T(4,128)(2,1)S(1)} %get-tuple-element.15), channel_id=1, source_target_pairs={{1,0},{2,1},{3,2},{4,3},{5,4},{6,5},{7,6},{8,7},{9,8},{10,9},{11,1... | collective-permute-start | bytes 98312 | tf_op jit(solution)/shard_map/ppermute | solution.py:230
  14.4 0.0 copy-start.4
  14.4 0.9 %copy-done.4 = bf16[32,4096]{1,0:T(8,128)(2,1)S(1)} copy-done((bf16[32,4096]{1,0:T(8,128)(2,1)S(1)}, bf16[32,4096]{1,0:T(8,128)(2,1)}, u32[]{:S(2)}) %copy-start.4) | copy-done | bytes 262168
  15.3 0.0 copy-start.5
  15.3 0.9 %copy-done.5 = bf16[1,32,4096]{2,1,0:T(8,128)(2,1)S(1)} copy-done((bf16[1,32,4096]{2,1,0:T(8,128)(2,1)S(1)}, bf16[1,32,4096]{2,1,0:T(8,128)(2,1)}, u32[]{:S(2)}) %copy-start.5) | copy-done | bytes 262168
  16.3 0.0 copy-start.8
  16.3 0.7 copy-done.8
  16.9 0.0 copy-start.9
  16.9 0.7 copy-done.9
  17.6 1.3 %shard_map.109 = (bf16[256,512]{1,0:T(8,128)(2,1)S(1)}, f32[16,4096]{1,0:T(8,128)S(1)}) custom-call(s32[1,512]{1,0:T(1,128)S(1)} %bitcast.23, s32[1,512]{1,0:T(1,128)S(1)} %bitcast.24, bf16[32,4096]{1,0:T(8,128)(2,1)S(1)} %bitcast.20, bf16[32,4096]{1,0:T(8,128)(2,1)S(1)} %copy-done.4), custom_call_target="tpu_custom_call" | custom-call | flops 134217728 | bytes 2097152 | tf_op jit(solution)/shard_map/pallas_call | solution.py:210
  18.9 0.0 copy-start.1
  18.9 0.0 collective-permute-done.above
  18.9 0.0 collective-permute-done.1.below
  18.9 0.0 copy-done.3
  18.9 1.3 %shard_map.110 = bf16[512,256]{1,0:T(8,128)(2,1)} custom-call(bf16[4,4096]{1,0:T(4,128)(2,1)S(1)} %collective-permute-done.above, bf16[4,4096]{1,0:T(4,128)(2,1)S(1)} %collective-permute-done.1.below, bf16[256,512]{1,0:T(8,128)(2,1)S(1)} %get-tuple-element.10.filled, f32[16,4096]{1,0:T(8,128)S(1)} %get-tuple-element.11.edges, bf16[512,512]{1,0:T(8,128)(2,1)S(1)} %copy-done.3), custom_call_target="tpu_custom_call" | custom-call | flops 134217728 | bytes 2097152 | tf_op jit(solution)/shard_map/pallas_call | solution.py:210
  20.2 0.0 copy-start.7
  20.2 12.5 %all-to-all-start = ((bf16[64,8,256]{2,1,0:T(8,128)(2,1)}), bf16[64,8,256]{2,1,0:T(8,128)(2,1)S(1)}, u32[]{:S(2)}, u32[]{:S(2)}) async-start(bf16[64,8,256]{2,1,0:T(8,128)(2,1)} %bitcast.7), calls=%async_computation | async-start | bytes 524288 | tf_op jit(solution)/shard_map/all_to_all | solution.py:279
  32.8 0.0 copy-start.10
  32.8 0.1 pad_add_fusion.place
  32.9 0.0 copy-done.7
  32.9 0.6 copy-done.10
  33.4 0.8 shard_map.111
  34.2 5.7 %collective-permute-start.2 = (f32[8,512]{1,0:T(8,128)S(1)}, f32[8,512]{1,0:T(8,128)S(1)}, u32[]{:S(2)}, u32[]{:S(2)}) collective-permute-start(f32[8,512]{1,0:T(8,128)S(1)} %get-tuple-element.13), channel_id=1, source_target_pairs={{0,63},{1,62},{2,61},{3,60},{4,59},{5,58},{6,57},{7,56},{8,55},{9,... | collective-permute-start | bytes 49160 | tf_op jit(solution)/shard_map/ppermute | solution.py:243
  39.9 3.7 %collective-permute-start.3 = (f32[2,512]{1,0:T(2,128)S(1)}, f32[2,512]{1,0:T(2,128)S(1)}, u32[]{:S(2)}, u32[]{:S(2)}) collective-permute-start(f32[2,512]{1,0:T(2,128)S(1)} %get-tuple-element.14), channel_id=1, source_target_pairs={{1,0},{2,1},{3,2},{4,3},{5,4},{6,5},{7,6},{8,7},{9,8},{10,9},{11,1... | collective-permute-start | bytes 12296 | tf_op jit(solution)/shard_map/ppermute | solution.py:244
  43.6 2.5 %collective-permute-done.3.following = f32[2,512]{1,0:T(2,128)S(1)} collective-permute-done((f32[2,512]{1,0:T(2,128)S(1)}, f32[2,512]{1,0:T(2,128)S(1)}, u32[]{:S(2)}, u32[]{:S(2)}) %collective-permute-start.3) | collective-permute-done | bytes 4128 | tf_op jit(solution)/shard_map/ppermute | solution.py:244
  46.1 1.1 %collective-permute-done.2.mirror = f32[8,512]{1,0:T(8,128)S(1)} collective-permute-done((f32[8,512]{1,0:T(8,128)S(1)}, f32[8,512]{1,0:T(8,128)S(1)}, u32[]{:S(2)}, u32[]{:S(2)}) %collective-permute-start.2) | collective-permute-done | bytes 16416 | tf_op jit(solution)/shard_map/ppermute | solution.py:243
  47.2 5.3 %all-to-all-done = bf16[64,8,256]{2,1,0:T(8,128)(2,1)S(1)} async-done(((bf16[64,8,256]{2,1,0:T(8,128)(2,1)}), bf16[64,8,256]{2,1,0:T(8,128)(2,1)S(1)}, u32[]{:S(2)}, u32[]{:S(2)}) %all-to-all-start) | async-done | bytes 262176 | tf_op jit(solution)/shard_map/all_to_all | solution.py:279
  52.6 0.0 copy-done.1
  52.6 0.0 copy-start
  52.6 1.1 %shard_map.112 = bf16[256,512]{1,0:T(8,128)(2,1)S(1)} custom-call(s32[2]{0:T(128)S(1)} %pad_add_fusion.place, bf16[512,256]{1,0:T(8,128)(2,1)S(1)} %bitcast.17, f32[8,512]{1,0:T(8,128)S(1)} %get-tuple-element.12.weight, f32[8,512]{1,0:T(8,128)S(1)} %collective-permute-done.2.mirror, f32[2,512]{1,0:T(2,128)S(1)} %collective-permute-done.3.following, ...), custom_call_target="tpu_custom_call" | custom-call | flops 268435456 | bytes 2097152 | tf_op jit(solution)/shard_map/pallas_call | solution.py:210
  53.7 0.0 copy-start.6
  53.7 11.9 %all_to_all.15 = bf16[8,32,512]{2,1,0:T(8,128)(2,1)S(1)} all-to-all(bf16[8,32,512]{2,1,0:T(8,128)(2,1)S(1)} %bitcast.18), channel_id=1, replica_groups=mesh['frac'=8,'tile'=64] {'frac'}, dimensions={0} | all-to-all | bytes 524288 | tf_op jit(solution)/shard_map/all_to_all | solution.py:294
  65.6 0.0 copy-done
  65.6 0.0 copy-done.6
  65.6 0.0 copy-start.2
  65.6 0.6 shard_map.113
  66.3 21.8 %all_to_all.16 = bf16[64,2,128]{2,1,0:T(2,128)(2,1)S(1)} all-to-all(bf16[64,2,128]{2,1,0:T(2,128)(2,1)S(1)} %bitcast.21), channel_id=1, replica_groups=mesh['frac'=8,'tile'=64] {'tile'}, dimensions={0} | all-to-all | bytes 65536 | tf_op jit(solution)/shard_map/all_to_all | solution.py:306
  88.0 0.0 copy-done.2
  88.0 0.9 %shard_map.114 = f32[4,8,512]{2,1,0:T(8,128)} custom-call(bf16[128,128]{1,0:T(8,128)(2,1)S(1)} %bitcast.22, bf16[4,128,512]{2,1,0:T(8,128)(2,1)S(1)} %copy-done.2), custom_call_target="tpu_custom_call" | custom-call | flops 67108864 | bytes 2097152 | tf_op jit(solution)/shard_map/pallas_call | solution.py:210
Async XLA Ops:
  0.0 18.9 %copy-start.3 = (bf16[512,512]{1,0:T(8,128)(2,1)S(1)}, bf16[512,512]{1,0:T(8,128)(2,1)}, u32[]{:S(2)}) copy-start(bf16[512,512]{1,0:T(8,128)(2,1)} %constant.19.clone.table) | copy-start | bytes 1572868
  1.1 17.9 %collective-permute-start = (bf16[4,4096]{1,0:T(4,128)(2,1)S(1)}, bf16[4,4096]{1,0:T(4,128)(2,1)S(1)}, u32[]{:S(2)}, u32[]{:S(2)}) collective-permute-start(bf16[4,4096]{1,0:T(4,128)(2,1)S(1)} %get-tuple-element.16), channel_id=1, source_target_pairs={{0,1},{1,2},{2,3},{3,4},{4,5},{5,6},{6,7},{7,8},{8,9},{9,10},{10,1... | collective-permute-start | bytes 98312 | tf_op jit(solution)/shard_map/ppermute | solution.py:229
  4.9 14.0 %collective-permute-start.1 = (bf16[4,4096]{1,0:T(4,128)(2,1)S(1)}, bf16[4,4096]{1,0:T(4,128)(2,1)S(1)}, u32[]{:S(2)}, u32[]{:S(2)}) collective-permute-start(bf16[4,4096]{1,0:T(4,128)(2,1)S(1)} %get-tuple-element.15), channel_id=1, source_target_pairs={{1,0},{2,1},{3,2},{4,3},{5,4},{6,5},{7,6},{8,7},{9,8},{10,9},{11,1... | collective-permute-start | bytes 98312 | tf_op jit(solution)/shard_map/ppermute | solution.py:230
  14.4 1.0 %copy-start.4 = (bf16[32,4096]{1,0:T(8,128)(2,1)S(1)}, bf16[32,4096]{1,0:T(8,128)(2,1)}, u32[]{:S(2)}) copy-start(bf16[32,4096]{1,0:T(8,128)(2,1)} %gain_in.1) | copy-start | bytes 786436
  15.3 0.9 %copy-start.5 = (bf16[1,32,4096]{2,1,0:T(8,128)(2,1)S(1)}, bf16[1,32,4096]{2,1,0:T(8,128)(2,1)}, u32[]{:S(2)}) copy-start(bf16[1,32,4096]{2,1,0:T(8,128)(2,1)} %param.11) | copy-start | bytes 786436
  16.3 0.7 copy-start.8
  16.9 0.7 copy-start.9
  18.9 33.7 %copy-start.1 = (bf16[512,1024]{1,0:T(8,128)(2,1)S(1)}, bf16[512,1024]{1,0:T(8,128)(2,1)}, u32[]{:S(2)}) copy-start(bf16[512,1024]{1,0:T(8,128)(2,1)} %constant.20.clone.table) | copy-start | bytes 3145732
  20.2 12.7 %copy-start.7 = (f32[8,8,512]{2,1,0:T(8,128)S(1)}, f32[8,8,512]{2,1,0:T(8,128)}, u32[]{:S(2)}) copy-start(f32[8,8,512]{2,1,0:T(8,128)} %filters.1) | copy-start | bytes 393220
  20.2 32.3 %all-to-all-start = ((bf16[64,8,256]{2,1,0:T(8,128)(2,1)}), bf16[64,8,256]{2,1,0:T(8,128)(2,1)S(1)}, u32[]{:S(2)}, u32[]{:S(2)}) async-start(bf16[64,8,256]{2,1,0:T(8,128)(2,1)} %bitcast.7), calls=%async_computation | async-start | bytes 524288 | tf_op jit(solution)/shard_map/all_to_all | solution.py:279
  32.8 0.7 copy-start.10
  34.2 13.0 %collective-permute-start.2 = (f32[8,512]{1,0:T(8,128)S(1)}, f32[8,512]{1,0:T(8,128)S(1)}, u32[]{:S(2)}, u32[]{:S(2)}) collective-permute-start(f32[8,512]{1,0:T(8,128)S(1)} %get-tuple-element.13), channel_id=1, source_target_pairs={{0,63},{1,62},{2,61},{3,60},{4,59},{5,58},{6,57},{7,56},{8,55},{9,... | collective-permute-start | bytes 49160 | tf_op jit(solution)/shard_map/ppermute | solution.py:243
  39.9 6.2 %collective-permute-start.3 = (f32[2,512]{1,0:T(2,128)S(1)}, f32[2,512]{1,0:T(2,128)S(1)}, u32[]{:S(2)}, u32[]{:S(2)}) collective-permute-start(f32[2,512]{1,0:T(2,128)S(1)} %get-tuple-element.14), channel_id=1, source_target_pairs={{1,0},{2,1},{3,2},{4,3},{5,4},{6,5},{7,6},{8,7},{9,8},{10,9},{11,1... | collective-permute-start | bytes 12296 | tf_op jit(solution)/shard_map/ppermute | solution.py:244
  52.6 13.1 %copy-start = (bf16[1024,512]{1,0:T(8,128)(2,1)S(1)}, bf16[1024,512]{1,0:T(8,128)(2,1)}, u32[]{:S(2)}) copy-start(bf16[1024,512]{1,0:T(8,128)(2,1)} %constant.22.clone.table) | copy-start | bytes 3145732
  53.7 12.0 %copy-start.6 = (bf16[256,256]{1,0:T(8,128)(2,1)S(1)}, bf16[256,256]{1,0:T(8,128)(2,1)}, u32[]{:S(2)}) copy-start(bf16[256,256]{1,0:T(8,128)(2,1)} %constant.21.clone.spread) | copy-start | bytes 393220
  65.6 22.4 %copy-start.2 = (bf16[4,128,512]{2,1,0:T(8,128)(2,1)S(1)}, bf16[4,128,512]{2,1,0:T(8,128)(2,1)}, u32[]{:S(2)}) copy-start(bf16[4,128,512]{2,1,0:T(8,128)(2,1)} %constant.23.clone.table) | copy-start | bytes 1572868

commit v2 on v1

--- a/solution.py
+++ b/solution.py
@@ -9,6 +9,7 @@
 
 N = 512
 RIM = 4
+MARK = 64.0
 TILES = 64
 HALF = TILES // 2
 FRACS = 8
@@ -39,7 +40,7 @@
 
 
 def forward_rows_table():
-    cosine, sine = wave(np.arange(N), np.arange(N))
+    cosine, sine = wave((np.arange(N) + RIM) % N, np.arange(N))
     return np.concatenate([cosine, sine], axis=1).astype(ml_dtypes.bfloat16)
 
 
@@ -87,55 +88,79 @@
     first_rows[1:2, :] = back[0:1]
 
 
-def fill_kernel(pixel_in, offset_in, frames_in, gain_in, filled, edges, pixel, offset, frames, gain, fill_map, extended, sems):
-    pairs = ((pixel_in, pixel), (offset_in, offset), (frames_in, frames), (gain_in, gain))
+def start_copies(pairs, sems):
     copies = [pltpu.make_async_copy(a, b, sems.at[i]) for i, (a, b) in enumerate(pairs)]
     for copy in copies:
         copy.start()
+    return copies
+
+
+def lane_hots(spot):
+    return (lax.broadcasted_iota(jnp.int32, (128, spot.shape[1]), 0) == (spot & 127)).astype(F32).astype(BF16)
+
+
+def own_rows_kernel(pixel_in, offset_in, frames_in, gain_in, sent, filled, tail, pixel, offset, frames, gain, fill_map, extended, sems):
+    pairs = ((pixel_in, pixel), (offset_in, offset), (frames_in, frames), (gain_in, gain))
+    copies = start_copies(pairs, sems)
     copies[0].wait()
     copies[1].wait()
     spot = pixel[...]
     step = offset[...].astype(F32)
-    row_key = ((spot >> 7) & 31) * ROWS + (spot >> 12)
-    lane_hot = (lax.broadcasted_iota(jnp.int32, (128, spot.shape[1]), 0) == (spot & 127)).astype(F32).astype(BF16)
+    key = ((spot >> 7) & 31) * ROWS + (spot >> 12)
+    lane_hot = lane_hots(spot)
     for part in range(4):
         rows = lax.broadcasted_iota(jnp.int32, (256, spot.shape[1]), 0) + 256 * part
-        row_hot = jnp.where(rows == row_key, step, 0.0).astype(BF16)
+        row_hot = jnp.where(rows == key, step, 0.0).astype(BF16)
         found = dot(row_hot, lane_hot, (1, 1))
         for i in range(8):
             lane = (part * 8 + i) * 128
             fill_map[:, lane : lane + 128] = found[i * ROWS : (i + 1) * ROWS]
     copies[2].wait()
     copies[3].wait()
-    extended[0:8, :] = jnp.zeros((8, N), F32)
-    extended[8 + ROWS : 16 + ROWS, :] = jnp.zeros((8, N), F32)
+    zero = jnp.zeros((8, N), F32)
+    row = lax.broadcasted_iota(jnp.int32, (8, N), 0)
     for c in range(COLS):
         lanes = slice(c * N, (c + 1) * N)
-        value = frames[:, lanes].astype(F32) * gain[:, lanes].astype(F32)
-        extended[8 : 8 + ROWS, :] = value
+        corrected = frames[:, lanes].astype(F32) * gain[:, lanes].astype(F32)
+        extended[0:8, :] = zero
+        extended[8 : 8 + ROWS, :] = corrected
+        extended[8 + ROWS : 16 + ROWS, :] = zero
         wanted = fill_map[:, lanes]
-        edges[0:8, lanes] = wanted[0:8]
-        edges[8:16, lanes] = wanted[ROWS - 8 : ROWS]
+        value = corrected
         for step in range(-RIM, RIM + 1):
             if step != 0:
                 value = jnp.where(wanted == step, extended[8 + step : 8 + step + ROWS, :], value)
-        filled[c * ROWS : (c + 1) * ROWS, :] = value.astype(BF16)
-
-
-def columns_kernel(above, below, filled, edges, table, out, halo, operand):
-    halo[...] = jnp.zeros(halo.shape, F32)
-    halo[4:8, :] = above[...].astype(F32)
-    halo[24:28, :] = below[...].astype(F32)
+        first = jnp.where(row.astype(F32) + wanted[0:8] < 0.0, MARK + wanted[0:8], value[0:8])
+        late = jnp.where(row.astype(F32) + wanted[ROWS - 8 :] > 7.0, wanted[ROWS - 8 :], 0.0)
+        extended[0:4, :] = corrected[0:4]
+        extended[4:8, :] = first[0:4]
+        extended[8 : 8 + ROWS, :] = value
+        extended[8 + ROWS : 16 + ROWS, :] = late
+        sent[:, lanes] = extended[0:8, :].astype(BF16)
+        late = jnp.where(row < 4, extended[12 + ROWS : 20 + ROWS, :], 0.0)
+        tail[:, lanes] = jnp.concatenate([late, corrected[ROWS - 8 :]], axis=0).astype(BF16)
+        window = extended[8 + RIM : 8 + RIM + ROWS, :]
+        window = jnp.concatenate([window[: ROWS - 8], jnp.where(row < 4, window[ROWS - 8 :], 0.0)], axis=0)
+        filled[c * ROWS : (c + 1) * ROWS, :] = window.astype(BF16)
+
+
+def columns_kernel(following, filled, tail, table, out, extended, operand):
+    row = lax.broadcasted_iota(jnp.int32, (8, N), 0)
     for c in range(COLS):
         lanes = slice(c * N, (c + 1) * N)
-        top = jnp.zeros((8, N), F32)
-        bottom = jnp.zeros((8, N), F32)
-        for step in range(1, RIM + 1):
-            top = top + jnp.where(edges[0:8, lanes] == -step, halo[8 - step : 16 - step, lanes], 0.0)
-            bottom = bottom + jnp.where(edges[8:16, lanes] == step, halo[16 + step : 24 + step, lanes], 0.0)
-        rows = filled[c * ROWS : (c + 1) * ROWS, :].astype(F32)
-        rows = jnp.concatenate([rows[0:8] + top, rows[8 : ROWS - 8], rows[ROWS - 8 :] + bottom], axis=0)
-        operand[c * ROWS : (c + 1) * ROWS, :] = rows.astype(BF16)
+        given = following[:, lanes].astype(F32)
+        ends = tail[:, lanes].astype(F32)
+        extended[0:8, :] = ends[8:16]
+        extended[8:16, :] = given
+        before = filled[c * ROWS + 16 : (c + 1) * ROWS, :].astype(F32)
+        marked = (given > 0.5 * MARK) & (row >= 4)
+        wanted = jnp.where(marked, given - MARK, ends[0:8])
+        value = jnp.where(row < 4, before[8:16], given)
+        for step in range(-RIM, RIM + 1):
+            if step != 0:
+                value = jnp.where(wanted == step, extended[4 + step : 12 + step, :], value)
+        operand[c * ROWS : c * ROWS + 16, :] = filled[c * ROWS : c * ROWS + 16, :]
+        operand[c * ROWS + 16 : (c + 1) * ROWS, :] = jnp.concatenate([before[0:8], value], axis=0).astype(BF16)
     out[...] = dot(table[...], operand[...], (1, 1)).astype(BF16)
 
 
@@ -159,6 +184,7 @@
         pair[4 + k : 5 + k, :] = both
 
     group = lax.broadcasted_iota(jnp.int32, (16, 8, 128), 2) >> 5
+    wraps = lax.broadcasted_iota(jnp.int32, (8, 128), 1) >= 128 - RIM
     source = spectrum[...].astype(F32).reshape(4, 4, 4, 8, 2 * 128)
     for half in range(2):
         pieces = []
@@ -170,8 +196,9 @@
             for j in range(3):
                 found = jnp.where(group == j, pieces[j][(j - c) % 4].reshape(16, 8, 128), found)
             for a in range(4):
-                for quarter in range(4):
+                for quarter in range(3):
                     by_row[a * 8 + half * 4 + c, :, quarter * 128 : (quarter + 1) * 128] = found[a * 4 + quarter]
+                by_row[a * 8 + half * 4 + c, :, 384:] = jnp.where(wraps, found[(a - 1) % 4 * 4 + 3], found[a * 4 + 3])
     operand = by_row[...].reshape(256, N).astype(BF16)
     scale = pair[...][None]
     with_cosine = dot(operand, table[:, :N], (1, 0)).reshape(32, 8, N) * scale
@@ -203,17 +230,19 @@
     out[...] = image.reshape(4, 8, N)
 
 
-def call(kernel, outs, scratch, scalars, cost, *args, space=pltpu.VMEM):
-    smem = pl.BlockSpec(memory_space=pltpu.SMEM)
-    vmem = pl.BlockSpec(memory_space=pltpu.VMEM)
+def call(kernel, outs, scratch, scalars, cost, *args, vmem=None, limit=VMEM_LIMIT):
+    scalar = pl.BlockSpec(memory_space=pltpu.SMEM)
+    block = pl.BlockSpec(memory_space=pltpu.VMEM)
+    rest = len(args) - scalars
+    blocks = rest if vmem is None else vmem
     many = isinstance(outs, (list, tuple))
     return pl.pallas_call(
         kernel,
         out_shape=outs,
-        in_specs=[smem] * scalars + [pl.BlockSpec(memory_space=space)] * (len(args) - scalars),
-        out_specs=[vmem] * len(outs) if many else vmem,
+        in_specs=[scalar] * scalars + [block] * blocks + [pl.BlockSpec(memory_space=pl.ANY)] * (rest - blocks),
+        out_specs=[block] * len(outs) if many else block,
         scratch_shapes=scratch,
-        compiler_params=pltpu.CompilerParams(vmem_limit_bytes=VMEM_LIMIT),
+        compiler_params=pltpu.CompilerParams(vmem_limit_bytes=limit),
         cost_estimate=pl.CostEstimate(flops=cost, bytes_accessed=1 << 21, transcendentals=0),
     )(*args)
 
@@ -222,14 +251,28 @@
     frames = frames.reshape(ROWS, WIDTH)
     place = jnp.stack([lax.axis_index("frac"), lax.axis_index("tile")]).astype(jnp.int32)
 
-    def edge(rows):
-        return (frames[rows].astype(F32) * gain[rows].astype(F32)).astype(BF16)
-
-    up = [(i, i + 1) for i in range(TILES - 1)]
-    above = lax.ppermute(edge(slice(ROWS - RIM, ROWS)), "tile", up)
-    below = lax.ppermute(edge(slice(0, RIM)), "tile", [(b, a) for a, b in up])
-
     shape = jax.ShapeDtypeStruct
+    defects = defect_pixel.shape[0]
+    block = (defect_pixel.reshape(1, -1), defect_offset.reshape(1, -1), frames, gain)
+    sent, filled, tail = call(
+        own_rows_kernel,
+        [pltpu.VMEM((8, WIDTH), BF16), pltpu.VMEM((COLS * ROWS, N), BF16), pltpu.VMEM((16, WIDTH), BF16)],
+        [
+            pltpu.VMEM((1, defects), jnp.int32),
+            pltpu.VMEM((1, defects), jnp.int32),
+            pltpu.VMEM((ROWS, WIDTH), BF16),
+            pltpu.VMEM((ROWS, WIDTH), BF16),
+            pltpu.VMEM((ROWS, WIDTH), F32),
+            pltpu.VMEM((ROWS + 24, N), F32),
+            pltpu.SemaphoreType.DMA((4,)),
+        ],
+        0,
+        1 << 27,
+        *(pltpu.with_memory_space_constraint(x, pltpu.HBM) for x in block),
+        vmem=0,
+        limit=None,
+    )
+    following_rows = lax.ppermute(sent, "tile", [((t + 1) % TILES, t) for t in range(TILES)])
     weight, mirror, first_rows = call(
         weights_kernel,
         [shape((8, N), F32), shape((8, N), F32), shape((2, N), F32)],
@@ -243,37 +286,15 @@
     mirror = lax.ppermute(mirror, "tile", [(t, TILES - 1 - t) for t in range(TILES)])
     following = lax.ppermute(first_rows, "tile", [((t + 1) % HALF, t) for t in range(HALF)])
 
-    defects = defect_pixel.shape[0]
-    filled, edges = call(
-        fill_kernel,
-        [shape((COLS * ROWS, N), BF16), shape((16, WIDTH), F32)],
-        [
-            pltpu.VMEM((1, defects), jnp.int32),
-            pltpu.VMEM((1, defects), jnp.int32),
-            pltpu.VMEM((ROWS, WIDTH), BF16),
-            pltpu.VMEM((ROWS, WIDTH), BF16),
-            pltpu.VMEM((ROWS, WIDTH), F32),
-            pltpu.VMEM((ROWS + 16, N), F32),
-            pltpu.SemaphoreType.DMA((4,)),
-        ],
-        0,
-        1 << 27,
-        defect_pixel.reshape(1, -1),
-        defect_offset.reshape(1, -1),
-        frames,
-        gain,
-        space=pltpu.HBM,
-    )
     columns = call(
         columns_kernel,
         shape((N, COLS * ROWS), BF16),
-        [pltpu.VMEM((32, WIDTH), F32), pltpu.VMEM((COLS * ROWS, N), BF16)],
+        [pltpu.VMEM((16, N), F32), pltpu.VMEM((COLS * ROWS, N), BF16)],
         0,
         1 << 27,
-        above,
-        below,
+        following_rows,
         filled,
-        edges,
+        tail,
         jnp.asarray(forward_columns_table()),
     )
     columns = lax.all_to_all(columns.reshape(TILES, 8, COLS * ROWS), "tile", 0, 0, tiled=True)

time: 89.4 us -> 84.8 us (0.949)
  local copies, waits for them, and re-layouts: 3.86 us -> 0.6 us
  starting transfers between devices: 35.2 us -> 32.5 us
  waiting for transfers between devices: 8.97 us -> 10.3 us
  other arithmetic: 1.12 us -> 0.08 us
    unnamed x22 -> x14, local copies, waits for them, and re-layouts: 3.86 us -> 0.6 us
    ppermute x2 -> x1, waiting for transfers between devices: 0.01 us -> 1.88 us  [per_device(): lax.ppermute(sent, 'tile', [((t + 1) % TILES, t) for t in range(TILES)])]
    ppermute x2 -> x1, starting transfers between devices: 13.3 us -> 11.5 us  [per_device(): lax.ppermute(sent, 'tile', [((t + 1) % TILES, t) for t in range(TILES)])]
    convert_element_type x1 -> x0, other arithmetic: 1.05 us -> none  [edge(): return (frames[rows].astype(F32) * gain[rows].astype(F32)).astype(BF16)]
  transfers between devices with their start and end apart: 5 -> 4, of which waited for: 3 -> 4; matrix products, arithmetic and copies ran while one was open for 0% -> 0% of each run, Pallas kernels for 2% -> 1%
where the time goes in v2:
time: 84.8 us; the launch traced here: 84.4 us
  blocking collectives  34.1 us (40%)
  starting transfers between devices  32.5 us (38%)
  waiting for transfers between devices  10.3 us (12%)
  Pallas kernels  6.71 us (8%)
    all_to_all x1, blocking collectives, per_device(): back = lax.all_to_all(back.reshape(TILES, 2, 128), 'tile', 0, 0, tiled=True)  22.2 us
    all_to_all x1, blocking collectives, per_device(): lax.all_to_all(weighted.reshape(FRACS, 32, N), 'frac', 0, 0, tiled=True)  11.9 us
    all_to_all x1, starting transfers between devices, per_device(): lax.all_to_all(columns.reshape(TILES, 8, COLS * ROWS), 'tile', 0, 0, tile...  11.7 us
    ppermute x1, starting transfers between devices, per_device(): lax.ppermute(sent, 'tile', [((t + 1) % TILES, t) for t in range(TILES)])  11.5 us
    pallas_call x6, Pallas kernels, call(): pl.pallas_call(kernel, out_shape=outs, in_specs=[scalar] * scalars + [blo...  6.71 us
    ppermute x1, starting transfers between devices, per_device(): lax.ppermute(mirror, 'tile', [(t, TILES - 1 - t) for t in range(TILES)])  5.67 us
    all_to_all x1, waiting for transfers between devices, per_device(): lax.all_to_all(columns.reshape(TILES, 8, COLS * ROWS), 'tile', 0, 0, tile...  5.35 us
    ppermute x1, starting transfers between devices, per_device(): lax.ppermute(first_rows, 'tile', [((t + 1) % HALF, t) for t in range(HALF)])  3.69 us
  transfers between devices with their start and end apart: 4, of which 4 were waited for; matrix products, arithmetic and copies ran while one was open for 0% of the time, Pallas kernels for 1%

profile of v2, /device:TPU:2, one launch (start us, length us, event | category | flops | bytes accessed | tf_op | source)
XLA Modules:
  0.0 84.4 jit_solution(16008421616938145874)
XLA Ops:
  0.0 0.0 copy-start.3
  0.0 2.1 %shard_map.109 = (bf16[8,4096]{1,0:T(8,128)(2,1)S(1)}, bf16[256,512]{1,0:T(8,128)(2,1)S(1)}, bf16[16,4096]{1,0:T(8,128)(2,1)S(1)}) custom-call(s32[1,512]{1,0:T(1,128)} %bitcast.17, s32[1,512]{1,0:T(1,128)} %bitcast.18, bf16[32,4096]{1,0:T(8,128)(2,1)} %bitcast.16, bf16[32,4096]{1,0:T(8,128)(2,1)} %gain_in.1), custom_call_target="tpu_custom_call" | custom-call | flops 134217728 | bytes 2097152 | tf_op jit(solution)/shard_map/pallas_call | solution.py:239
  2.1 0.0 copy-start.1
  2.2 11.5 %collective-permute-start = (bf16[8,4096]{1,0:T(8,128)(2,1)S(1)}, bf16[8,4096]{1,0:T(8,128)(2,1)S(1)}, u32[]{:S(2)}, u32[]{:S(2)}) collective-permute-start(bf16[8,4096]{1,0:T(8,128)(2,1)S(1)} %get-tuple-element.11), channel_id=1, source_target_pairs={{1,0},{2,1},{3,2},{4,3},{5,4},{6,5},{7,6},{8,7},{9,8},{10,9},{11,1... | collective-permute-start | bytes 196616 | tf_op jit(solution)/shard_map/ppermute | solution.py:275
  13.7 1.9 %collective-permute-done.following = bf16[8,4096]{1,0:T(8,128)(2,1)S(1)} collective-permute-done((bf16[8,4096]{1,0:T(8,128)(2,1)S(1)}, bf16[8,4096]{1,0:T(8,128)(2,1)S(1)}, u32[]{:S(2)}, u32[]{:S(2)}) %collective-permute-start) | collective-permute-done | bytes 65568 | tf_op jit(solution)/shard_map/ppermute | solution.py:275
  15.6 0.0 copy-done.3
  15.6 1.2 %shard_map.110 = bf16[512,256]{1,0:T(8,128)(2,1)} custom-call(bf16[8,4096]{1,0:T(8,128)(2,1)S(1)} %collective-permute-done.following, bf16[256,512]{1,0:T(8,128)(2,1)S(1)} %get-tuple-element.12.filled, bf16[16,4096]{1,0:T(8,128)(2,1)S(1)} %get-tuple-element.13.tail, bf16[512,512]{1,0:T(8,128)(2,1)S(1)} %copy-done.3), custom_call_target="tpu_custom_call" | custom-call | flops 134217728 | bytes 2097152 | tf_op jit(solution)/shard_map/pallas_call | solution.py:239
  16.7 0.0 copy-start.5
  16.7 11.7 %all-to-all-start = ((bf16[64,8,256]{2,1,0:T(8,128)(2,1)}), bf16[64,8,256]{2,1,0:T(8,128)(2,1)S(1)}, u32[]{:S(2)}, u32[]{:S(2)}) async-start(bf16[64,8,256]{2,1,0:T(8,128)(2,1)} %bitcast.5), calls=%async_computation | async-start | bytes 524288 | tf_op jit(solution)/shard_map/all_to_all | solution.py:300
  28.4 0.0 copy-start.6
  28.4 0.1 pad_add_fusion.place
  28.5 0.0 copy-done.5
  28.5 0.6 copy-done.6
  29.1 0.8 shard_map.111
  29.9 5.7 %collective-permute-start.1 = (f32[8,512]{1,0:T(8,128)S(1)}, f32[8,512]{1,0:T(8,128)S(1)}, u32[]{:S(2)}, u32[]{:S(2)}) collective-permute-start(f32[8,512]{1,0:T(8,128)S(1)} %get-tuple-element.15), channel_id=1, source_target_pairs={{0,63},{1,62},{2,61},{3,60},{4,59},{5,58},{6,57},{7,56},{8,55},{9,... | collective-permute-start | bytes 49160 | tf_op jit(solution)/shard_map/ppermute | solution.py:286
  35.5 3.7 %collective-permute-start.2 = (f32[2,512]{1,0:T(2,128)S(1)}, f32[2,512]{1,0:T(2,128)S(1)}, u32[]{:S(2)}, u32[]{:S(2)}) collective-permute-start(f32[2,512]{1,0:T(2,128)S(1)} %get-tuple-element.16), channel_id=1, source_target_pairs={{1,0},{2,1},{3,2},{4,3},{5,4},{6,5},{7,6},{8,7},{9,8},{10,9},{11,1... | collective-permute-start | bytes 12296 | tf_op jit(solution)/shard_map/ppermute | solution.py:287
  39.2 2.3 %collective-permute-done.2.following = f32[2,512]{1,0:T(2,128)S(1)} collective-permute-done((f32[2,512]{1,0:T(2,128)S(1)}, f32[2,512]{1,0:T(2,128)S(1)}, u32[]{:S(2)}, u32[]{:S(2)}) %collective-permute-start.2) | collective-permute-done | bytes 4128 | tf_op jit(solution)/shard_map/ppermute | solution.py:287
  41.6 0.7 collective-permute-done.1.mirror
  42.3 5.3 %all-to-all-done = bf16[64,8,256]{2,1,0:T(8,128)(2,1)S(1)} async-done(((bf16[64,8,256]{2,1,0:T(8,128)(2,1)}), bf16[64,8,256]{2,1,0:T(8,128)(2,1)S(1)}, u32[]{:S(2)}, u32[]{:S(2)}) %all-to-all-start) | async-done | bytes 262176 | tf_op jit(solution)/shard_map/all_to_all | solution.py:300
  47.6 0.0 copy-done.1
  47.6 0.0 copy-start
  47.6 1.1 %shard_map.112 = bf16[256,512]{1,0:T(8,128)(2,1)S(1)} custom-call(s32[2]{0:T(128)S(1)} %pad_add_fusion.place, bf16[512,256]{1,0:T(8,128)(2,1)S(1)} %bitcast.11, f32[8,512]{1,0:T(8,128)S(1)} %get-tuple-element.14.weight, f32[8,512]{1,0:T(8,128)S(1)} %collective-permute-done.1.mirror, f32[2,512]{1,0:T(2,128)S(1)} %collective-permute-done.2.following, ...), custom_call_target="tpu_custom_call" | custom-call | flops 268435456 | bytes 2097152 | tf_op jit(solution)/shard_map/pallas_call | solution.py:239
  48.7 0.0 copy-start.4
  48.8 11.9 %all_to_all.15 = bf16[8,32,512]{2,1,0:T(8,128)(2,1)S(1)} all-to-all(bf16[8,32,512]{2,1,0:T(8,128)(2,1)S(1)} %bitcast.12), channel_id=1, replica_groups=mesh['frac'=8,'tile'=64] {'frac'}, dimensions={0} | all-to-all | bytes 524288 | tf_op jit(solution)/shard_map/all_to_all | solution.py:315
  60.7 0.0 copy-done
  60.7 0.0 copy-done.4
  60.7 0.0 copy-start.2
  60.7 0.6 shard_map.113
  61.3 22.2 %all_to_all.16 = bf16[64,2,128]{2,1,0:T(2,128)(2,1)S(1)} all-to-all(bf16[64,2,128]{2,1,0:T(2,128)(2,1)S(1)} %bitcast.14), channel_id=1, replica_groups=mesh['frac'=8,'tile'=64] {'tile'}, dimensions={0} | all-to-all | bytes 65536 | tf_op jit(solution)/shard_map/all_to_all | solution.py:327
  83.5 0.0 copy-done.2
  83.5 0.9 %shard_map.114 = f32[4,8,512]{2,1,0:T(8,128)} custom-call(bf16[128,128]{1,0:T(8,128)(2,1)S(1)} %bitcast.15, bf16[4,128,512]{2,1,0:T(8,128)(2,1)S(1)} %copy-done.2), custom_call_target="tpu_custom_call" | custom-call | flops 67108864 | bytes 2097152 | tf_op jit(solution)/shard_map/pallas_call | solution.py:239
Async XLA Ops:
  0.0 15.6 %copy-start.3 = (bf16[512,512]{1,0:T(8,128)(2,1)S(1)}, bf16[512,512]{1,0:T(8,128)(2,1)}, u32[]{:S(2)}) copy-start(bf16[512,512]{1,0:T(8,128)(2,1)} %constant.19.clone.table) | copy-start | bytes 1572868
  2.1 45.5 %copy-start.1 = (bf16[512,1024]{1,0:T(8,128)(2,1)S(1)}, bf16[512,1024]{1,0:T(8,128)(2,1)}, u32[]{:S(2)}) copy-start(bf16[512,1024]{1,0:T(8,128)(2,1)} %constant.20.clone.table) | copy-start | bytes 3145732
  2.2 13.4 %collective-permute-start = (bf16[8,4096]{1,0:T(8,128)(2,1)S(1)}, bf16[8,4096]{1,0:T(8,128)(2,1)S(1)}, u32[]{:S(2)}, u32[]{:S(2)}) collective-permute-start(bf16[8,4096]{1,0:T(8,128)(2,1)S(1)} %get-tuple-element.11), channel_id=1, source_target_pairs={{1,0},{2,1},{3,2},{4,3},{5,4},{6,5},{7,6},{8,7},{9,8},{10,9},{11,1... | collective-permute-start | bytes 196616 | tf_op jit(solution)/shard_map/ppermute | solution.py:275
  16.7 11.8 %copy-start.5 = (f32[8,8,512]{2,1,0:T(8,128)S(1)}, f32[8,8,512]{2,1,0:T(8,128)}, u32[]{:S(2)}) copy-start(f32[8,8,512]{2,1,0:T(8,128)} %filters.1) | copy-start | bytes 393220
  16.7 30.9 %all-to-all-start = ((bf16[64,8,256]{2,1,0:T(8,128)(2,1)}), bf16[64,8,256]{2,1,0:T(8,128)(2,1)S(1)}, u32[]{:S(2)}, u32[]{:S(2)}) async-start(bf16[64,8,256]{2,1,0:T(8,128)(2,1)} %bitcast.5), calls=%async_computation | async-start | bytes 524288 | tf_op jit(solution)/shard_map/all_to_all | solution.py:300
  28.4 0.7 copy-start.6
  29.9 12.4 %collective-permute-start.1 = (f32[8,512]{1,0:T(8,128)S(1)}, f32[8,512]{1,0:T(8,128)S(1)}, u32[]{:S(2)}, u32[]{:S(2)}) collective-permute-start(f32[8,512]{1,0:T(8,128)S(1)} %get-tuple-element.15), channel_id=1, source_target_pairs={{0,63},{1,62},{2,61},{3,60},{4,59},{5,58},{6,57},{7,56},{8,55},{9,... | collective-permute-start | bytes 49160 | tf_op jit(solution)/shard_map/ppermute | solution.py:286
  35.5 6.0 %collective-permute-start.2 = (f32[2,512]{1,0:T(2,128)S(1)}, f32[2,512]{1,0:T(2,128)S(1)}, u32[]{:S(2)}, u32[]{:S(2)}) collective-permute-start(f32[2,512]{1,0:T(2,128)S(1)} %get-tuple-element.16), channel_id=1, source_target_pairs={{1,0},{2,1},{3,2},{4,3},{5,4},{6,5},{7,6},{8,7},{9,8},{10,9},{11,1... | collective-permute-start | bytes 12296 | tf_op jit(solution)/shard_map/ppermute | solution.py:287
  47.6 13.1 %copy-start = (bf16[1024,512]{1,0:T(8,128)(2,1)S(1)}, bf16[1024,512]{1,0:T(8,128)(2,1)}, u32[]{:S(2)}) copy-start(bf16[1024,512]{1,0:T(8,128)(2,1)} %constant.22.clone.table) | copy-start | bytes 3145732
  48.7 12.0 %copy-start.4 = (bf16[256,256]{1,0:T(8,128)(2,1)S(1)}, bf16[256,256]{1,0:T(8,128)(2,1)}, u32[]{:S(2)}) copy-start(bf16[256,256]{1,0:T(8,128)(2,1)} %constant.21.clone.spread) | copy-start | bytes 393220
  60.7 22.8 %copy-start.2 = (bf16[4,128,512]{2,1,0:T(8,128)(2,1)S(1)}, bf16[4,128,512]{2,1,0:T(8,128)(2,1)}, u32[]{:S(2)}) copy-start(bf16[4,128,512]{2,1,0:T(8,128)(2,1)} %constant.23.clone.table) | copy-start | bytes 1572868

commit v3 on v2

--- a/solution.py
+++ b/solution.py
@@ -70,13 +70,61 @@
     return lax.dot_general(a, b, ((contract[:1], contract[1:]), ((), ())), preferred_element_type=F32)
 
 
-def weights_kernel(place, groups, filters, weight, mirror, first_rows):
+def start_copies(pairs, sems):
+    copies = [pltpu.make_async_copy(a, b, sems.at[i]) for i, (a, b) in enumerate(pairs)]
+    for copy in copies:
+        copy.start()
+    return copies
+
+
+def sent_rows_kernel(pixel_in, offset_in, frames_in, gain_in, sent, fill_map, pixel, offset, frames, gain, extended, sems):
+    pairs = ((pixel_in, pixel), (offset_in, offset), (frames_in.at[0:16], frames), (gain_in.at[0:16], gain))
+    copies = start_copies(pairs, sems)
+    copies[0].wait()
+    copies[1].wait()
+    spot = pixel[...]
+    step = offset[...].astype(F32)
+    key = ((spot >> 7) & 31) * ROWS + (spot >> 12)
+    lane_hot = (lax.broadcasted_iota(jnp.int32, (128, spot.shape[1]), 0) == (spot & 127)).astype(F32).astype(BF16)
+    for part in range(4):
+        rows = lax.broadcasted_iota(jnp.int32, (256, spot.shape[1]), 0) + 256 * part
+        row_hot = jnp.where(rows == key, step, 0.0).astype(BF16)
+        found = dot(row_hot, lane_hot, (1, 1)).astype(BF16)
+        for i in range(8):
+            lane = (part * 8 + i) * 128
+            fill_map[:, lane : lane + 128] = found[i * ROWS : (i + 1) * ROWS]
+    copies[2].wait()
+    copies[3].wait()
+    zero = jnp.zeros((8, N), F32)
+    row = lax.broadcasted_iota(jnp.int32, (8, N), 0).astype(F32)
+    for c in range(COLS):
+        lanes = slice(c * N, (c + 1) * N)
+        corrected = (frames[:, lanes].astype(F32) * gain[:, lanes].astype(F32))[0:8]
+        extended[0:8, :] = zero
+        extended[8:16, :] = corrected
+        extended[16:24, :] = zero
+        wanted = fill_map[0:16, lanes].astype(F32)[0:8]
+        value = corrected
+        for step in range(-RIM, RIM + 1):
+            if step != 0:
+                value = jnp.where(wanted == step, extended[8 + step : 16 + step, :], value)
+        value = jnp.where(row + wanted < 0.0, MARK + wanted, value)
+        extended[0:4, :] = corrected[0:4]
+        extended[4:8, :] = value[0:4]
+        sent[:, lanes] = extended[0:8, :].astype(BF16)
+
+
+def own_rows_kernel(fill_map, groups_in, filters_in, frames_in, gain_in, filled, tail, weight, mirror, first_rows, groups, filters, frames, gain, extended, sems):
+    pairs = ((groups_in, groups), (filters_in, filters), (frames_in, frames), (gain_in, gain))
+    copies = start_copies(pairs, sems)
+    turn = (lax.broadcasted_iota(jnp.int32, (N, N), 0) + lax.broadcasted_iota(jnp.int32, (N, N), 1)) & (N - 1)
+    turn = (turn == 0).astype(F32).astype(BF16)
+    copies[0].wait()
+    copies[1].wait()
     square = jnp.zeros(filters.shape[1:], F32)
     for f in range(FRACS):
         square = square + filters[groups[f]] * filters[groups[f]]
-    mine = filters[groups[place[0]]] / jnp.sqrt(square)
-    turn = (lax.broadcasted_iota(jnp.int32, (N, N), 0) + lax.broadcasted_iota(jnp.int32, (N, N), 1)) & (N - 1)
-    turn = (turn == 0).astype(F32).astype(BF16)
+    mine = filters[groups[lax.axis_index("frac")]] / jnp.sqrt(square)
     high = mine.astype(BF16)
     low = (mine - high.astype(F32)).astype(BF16)
     back = dot(high, turn, (1, 0)) + dot(low, turn, (1, 0))
@@ -87,34 +135,6 @@
     first_rows[0:1, :] = mine[0:1]
     first_rows[1:2, :] = back[0:1]
 
-
-def start_copies(pairs, sems):
-    copies = [pltpu.make_async_copy(a, b, sems.at[i]) for i, (a, b) in enumerate(pairs)]
-    for copy in copies:
-        copy.start()
-    return copies
-
-
-def lane_hots(spot):
-    return (lax.broadcasted_iota(jnp.int32, (128, spot.shape[1]), 0) == (spot & 127)).astype(F32).astype(BF16)
-
-
-def own_rows_kernel(pixel_in, offset_in, frames_in, gain_in, sent, filled, tail, pixel, offset, frames, gain, fill_map, extended, sems):
-    pairs = ((pixel_in, pixel), (offset_in, offset), (frames_in, frames), (gain_in, gain))
-    copies = start_copies(pairs, sems)
-    copies[0].wait()
-    copies[1].wait()
-    spot = pixel[...]
-    step = offset[...].astype(F32)
-    key = ((spot >> 7) & 31) * ROWS + (spot >> 12)
-    lane_hot = lane_hots(spot)
-    for part in range(4):
-        rows = lax.broadcasted_iota(jnp.int32, (256, spot.shape[1]), 0) + 256 * part
-        row_hot = jnp.where(rows == key, step, 0.0).astype(BF16)
-        found = dot(row_hot, lane_hot, (1, 1))
-        for i in range(8):
-            lane = (part * 8 + i) * 128
-            fill_map[:, lane : lane + 128] = found[i * ROWS : (i + 1) * ROWS]
     copies[2].wait()
     copies[3].wait()
     zero = jnp.zeros((8, N), F32)
@@ -125,18 +145,14 @@
         extended[0:8, :] = zero
         extended[8 : 8 + ROWS, :] = corrected
         extended[8 + ROWS : 16 + ROWS, :] = zero
-        wanted = fill_map[:, lanes]
+        wanted = fill_map[:, lanes].astype(F32)
         value = corrected
         for step in range(-RIM, RIM + 1):
             if step != 0:
                 value = jnp.where(wanted == step, extended[8 + step : 8 + step + ROWS, :], value)
-        first = jnp.where(row.astype(F32) + wanted[0:8] < 0.0, MARK + wanted[0:8], value[0:8])
         late = jnp.where(row.astype(F32) + wanted[ROWS - 8 :] > 7.0, wanted[ROWS - 8 :], 0.0)
-        extended[0:4, :] = corrected[0:4]
-        extended[4:8, :] = first[0:4]
         extended[8 : 8 + ROWS, :] = value
         extended[8 + ROWS : 16 + ROWS, :] = late
-        sent[:, lanes] = extended[0:8, :].astype(BF16)
         late = jnp.where(row < 4, extended[12 + ROWS : 20 + ROWS, :], 0.0)
         tail[:, lanes] = jnp.concatenate([late, corrected[ROWS - 8 :]], axis=0).astype(BF16)
         window = extended[8 + RIM : 8 + RIM + ROWS, :]
@@ -164,8 +180,8 @@
     out[...] = dot(table[...], operand[...], (1, 1)).astype(BF16)
 
 
-def rows_kernel(place, spectrum, weight, mirror, following, table, out, by_row, pair):
-    tile = place[1]
+def rows_kernel(spectrum, weight, mirror, following, table, out, by_row, pair):
+    tile = lax.axis_index("tile")
     lower = tile < HALF
     last = tile == HALF - 1
     for k in range(4):
@@ -230,58 +246,73 @@
     out[...] = image.reshape(4, 8, N)
 
 
-def call(kernel, outs, scratch, scalars, cost, *args, vmem=None, limit=VMEM_LIMIT):
-    scalar = pl.BlockSpec(memory_space=pltpu.SMEM)
+def call(kernel, outs, scratch, cost, *args, vmem=None):
     block = pl.BlockSpec(memory_space=pltpu.VMEM)
-    rest = len(args) - scalars
-    blocks = rest if vmem is None else vmem
+    blocks = len(args) if vmem is None else vmem
     many = isinstance(outs, (list, tuple))
     return pl.pallas_call(
         kernel,
         out_shape=outs,
-        in_specs=[scalar] * scalars + [block] * blocks + [pl.BlockSpec(memory_space=pl.ANY)] * (rest - blocks),
+        in_specs=[block] * blocks + [pl.BlockSpec(memory_space=pl.ANY)] * (len(args) - blocks),
         out_specs=[block] * len(outs) if many else block,
         scratch_shapes=scratch,
-        compiler_params=pltpu.CompilerParams(vmem_limit_bytes=limit),
+        compiler_params=pltpu.CompilerParams(vmem_limit_bytes=VMEM_LIMIT),
         cost_estimate=pl.CostEstimate(flops=cost, bytes_accessed=1 << 21, transcendentals=0),
     )(*args)
 
 
 def per_device(frames, gain, defect_pixel, defect_offset, fraction_group, exposure_filter):
     frames = frames.reshape(ROWS, WIDTH)
-    place = jnp.stack([lax.axis_index("frac"), lax.axis_index("tile")]).astype(jnp.int32)
 
     shape = jax.ShapeDtypeStruct
     defects = defect_pixel.shape[0]
-    block = (defect_pixel.reshape(1, -1), defect_offset.reshape(1, -1), frames, gain)
-    sent, filled, tail = call(
-        own_rows_kernel,
-        [pltpu.VMEM((8, WIDTH), BF16), pltpu.VMEM((COLS * ROWS, N), BF16), pltpu.VMEM((16, WIDTH), BF16)],
+    def stay(x):
+        return pltpu.with_memory_space_constraint(x, pltpu.HBM)
+
+    frames, gain = stay(frames), stay(gain)
+    sent, fill_map = call(
+        sent_rows_kernel,
+        [pltpu.VMEM((8, WIDTH), BF16), pltpu.VMEM((ROWS, WIDTH), BF16)],
         [
             pltpu.VMEM((1, defects), jnp.int32),
             pltpu.VMEM((1, defects), jnp.int32),
+            pltpu.VMEM((16, WIDTH), BF16),
+            pltpu.VMEM((16, WIDTH), BF16),
+            pltpu.VMEM((24, N), F32),
+            pltpu.SemaphoreType.DMA((4,)),
+        ],
+        1 << 27,
+        stay(defect_pixel.reshape(1, -1)),
+        stay(defect_offset.reshape(1, -1)),
+        frames,
+        gain,
+        vmem=0,
+    )
+    following_rows = lax.ppermute(sent, "tile", [((t + 1) % TILES, t) for t in range(TILES)])
+    filled, tail, weight, mirror, first_rows = call(
+        own_rows_kernel,
+        [
+            pltpu.VMEM((COLS * ROWS, N), BF16),
+            pltpu.VMEM((16, WIDTH), BF16),
+            pltpu.VMEM((8, N), F32),
+            pltpu.VMEM((8, N), F32),
+            pltpu.VMEM((2, N), F32),
+        ],
+        [
+            pltpu.SMEM((FRACS,), jnp.int32),
+            pltpu.VMEM((8, 8, N), F32),
             pltpu.VMEM((ROWS, WIDTH), BF16),
             pltpu.VMEM((ROWS, WIDTH), BF16),
-            pltpu.VMEM((ROWS, WIDTH), F32),
             pltpu.VMEM((ROWS + 24, N), F32),
             pltpu.SemaphoreType.DMA((4,)),
         ],
-        0,
         1 << 27,
-        *(pltpu.with_memory_space_constraint(x, pltpu.HBM) for x in block),
-        vmem=0,
-        limit=None,
-    )
-    following_rows = lax.ppermute(sent, "tile", [((t + 1) % TILES, t) for t in range(TILES)])
-    weight, mirror, first_rows = call(
-        weights_kernel,
-        [shape((8, N), F32), shape((8, N), F32), shape((2, N), F32)],
-        [],
-        2,
-        1 << 23,
-        place,
-        fraction_group,
-        exposure_filter,
+        fill_map,
+        stay(fraction_group),
+        stay(exposure_filter),
+        frames,
+        gain,
+        vmem=1,
     )
     mirror = lax.ppermute(mirror, "tile", [(t, TILES - 1 - t) for t in range(TILES)])
     following = lax.ppermute(first_rows, "tile", [((t + 1) % HALF, t) for t in range(HALF)])
@@ -290,7 +321,6 @@
         columns_kernel,
         shape((N, COLS * ROWS), BF16),
         [pltpu.VMEM((16, N), F32), pltpu.VMEM((COLS * ROWS, N), BF16)],
-        0,
         1 << 27,
         following_rows,
         filled,
@@ -303,9 +333,7 @@
         rows_kernel,
         shape((256, N), BF16),
         [pltpu.VMEM((32, 8, N), F32), pltpu.VMEM((8, N), F32)],
-        1,
         1 << 28,
-        place,
         columns.reshape(N, COLS * ROWS),
         weight,
         mirror,
@@ -318,7 +346,6 @@
         back_rows_kernel,
         shape((2 * TILES, 128), BF16),
         [pltpu.VMEM((2 * TILES, 128), F32)],
-        0,
         1 << 28,
         parts.reshape(256, N),
         jnp.asarray(sum_and_spread_table()),
@@ -330,7 +357,6 @@
         back_columns_kernel,
         shape((4, 8, N), F32),
         [],
-        0,
         1 << 26,
         back.reshape(2 * TILES, 128),
         jnp.asarray(inverse_columns_table()),

time: 84.8 us -> 83 us (0.979)
    ppermute x1, waiting for transfers between devices: 1.88 us -> 0.01 us  [per_device(): lax.ppermute(sent, 'tile', [((t + 1) % TILES, t) for t in range(TILES)])]
    ppermute x1, waiting for transfers between devices: 0.71 us -> 2.32 us  [per_device(): lax.ppermute(mirror, 'tile', [(t, TILES - 1 - t) for t in range(TILES)])]
  transfers between devices with their start and end apart: 4 -> 4, of which waited for: 4 -> 3; matrix products, arithmetic and copies ran while one was open for 0% -> 0% of each run, Pallas kernels for 1% -> 2%
where the time goes in v3:
time: 83 us; the launch traced here: 82.7 us
  blocking collectives  33.8 us (41%)
  starting transfers between devices  32.2 us (39%)
  waiting for transfers between devices  9.78 us (12%)
  Pallas kernels  6.8 us (8%)
    all_to_all x1, blocking collectives, per_device(): back = lax.all_to_all(back.reshape(TILES, 2, 128), 'tile', 0, 0, tiled=True)  21.8 us
    all_to_all x1, blocking collectives, per_device(): lax.all_to_all(weighted.reshape(FRACS, 32, N), 'frac', 0, 0, tiled=True)  12 us
    ppermute x1, starting transfers between devices, per_device(): lax.ppermute(sent, 'tile', [((t + 1) % TILES, t) for t in range(TILES)])  11.5 us
    all_to_all x1, starting transfers between devices, per_device(): lax.all_to_all(columns.reshape(TILES, 8, COLS * ROWS), 'tile', 0, 0, tile...  11.3 us
    pallas_call x6, Pallas kernels, call(): pl.pallas_call(kernel, out_shape=outs, in_specs=[block] * blocks + [pl.Bl...  6.8 us
    ppermute x1, starting transfers between devices, per_device(): lax.ppermute(mirror, 'tile', [(t, TILES - 1 - t) for t in range(TILES)])  5.68 us
    all_to_all x1, waiting for transfers between devices, per_device(): lax.all_to_all(columns.reshape(TILES, 8, COLS * ROWS), 'tile', 0, 0, tile...  5.3 us
    ppermute x1, starting transfers between devices, per_device(): lax.ppermute(first_rows, 'tile', [((t + 1) % HALF, t) for t in range(HALF)])  3.69 us
  transfers between devices with their start and end apart: 4, of which 3 were waited for; matrix products, arithmetic and copies ran while one was open for 0% of the time, Pallas kernels for 2%

profile of v3, /device:TPU:2, one launch (start us, length us, event | category | flops | bytes accessed | tf_op | source)
XLA Modules:
  0.0 82.7 jit_solution(16264333282615560700)
XLA Ops:
  0.0 1.5 %shard_map.109 = (bf16[8,4096]{1,0:T(8,128)(2,1)S(1)}, bf16[32,4096]{1,0:T(8,128)(2,1)S(1)}) custom-call(s32[1,512]{1,0:T(1,128)} %bitcast.16, s32[1,512]{1,0:T(1,128)} %bitcast.17, bf16[32,4096]{1,0:T(8,128)(2,1)} %bitcast.14, bf16[32,4096]{1,0:T(8,128)(2,1)} %gain_in.3), custom_call_target="tpu_custom_call" | custom-call | flops 134217728 | bytes 2097152 | tf_op jit(solution)/shard_map/pallas_call | solution.py:253
  1.5 0.0 copy-start.3
  1.5 11.5 %collective-permute-start = (bf16[8,4096]{1,0:T(8,128)(2,1)S(1)}, bf16[8,4096]{1,0:T(8,128)(2,1)S(1)}, u32[]{:S(2)}, u32[]{:S(2)}) collective-permute-start(bf16[8,4096]{1,0:T(8,128)(2,1)S(1)} %get-tuple-element.12), channel_id=1, source_target_pairs={{1,0},{2,1},{3,2},{4,3},{5,4},{6,5},{7,6},{8,7},{9,8},{10,9},{11,1... | collective-permute-start | bytes 196616 | tf_op jit(solution)/shard_map/ppermute | solution.py:291
  13.0 2.1 %shard_map.110 = (bf16[256,512]{1,0:T(8,128)(2,1)S(1)}, bf16[16,4096]{1,0:T(8,128)(2,1)S(1)}, f32[8,512]{1,0:T(8,128)S(1)}, f32[8,512]{1,0:T(8,128)S(1)}, f32[2,512]{1,0:T(2,128)S(1)}) custom-call(bf16[32,4096]{1,0:T(8,128)(2,1)S(1)} %get-tuple-element.13.fill_map, s32[8]{0:T(128)} %groups_in.1, f32[8,8,512]{2,1,0:T(8,128)} %filters_in.1, ...), custom_call_target="tpu_custom_call" | custom-call | flops 134217728 | bytes 2097152 | tf_op jit(solution)/shard_map/pallas_call | solution.py:253
  15.1 0.0 copy-start.1
  15.1 0.0 collective-permute-done.following
  15.1 0.0 copy-done.3
  15.1 1.2 %shard_map.111 = bf16[512,256]{1,0:T(8,128)(2,1)} custom-call(bf16[8,4096]{1,0:T(8,128)(2,1)S(1)} %collective-permute-done.following, bf16[256,512]{1,0:T(8,128)(2,1)S(1)} %get-tuple-element.14.filled, bf16[16,4096]{1,0:T(8,128)(2,1)S(1)} %get-tuple-element.15.tail, bf16[512,512]{1,0:T(8,128)(2,1)S(1)} %copy-done.3), custom_call_target="tpu_custom_call" | custom-call | flops 134217728 | bytes 2097152 | tf_op jit(solution)/shard_map/pallas_call | solution.py:253
  16.3 11.3 %all-to-all-start = ((bf16[64,8,256]{2,1,0:T(8,128)(2,1)}), bf16[64,8,256]{2,1,0:T(8,128)(2,1)S(1)}, u32[]{:S(2)}, u32[]{:S(2)}) async-start(bf16[64,8,256]{2,1,0:T(8,128)(2,1)} %bitcast.3), calls=%async_computation | async-start | bytes 524288 | tf_op jit(solution)/shard_map/all_to_all | solution.py:330
  27.6 5.7 %collective-permute-start.1 = (f32[8,512]{1,0:T(8,128)S(1)}, f32[8,512]{1,0:T(8,128)S(1)}, u32[]{:S(2)}, u32[]{:S(2)}) collective-permute-start(f32[8,512]{1,0:T(8,128)S(1)} %get-tuple-element.17), channel_id=1, source_target_pairs={{0,63},{1,62},{2,61},{3,60},{4,59},{5,58},{6,57},{7,56},{8,55},{9,... | collective-permute-start | bytes 49160 | tf_op jit(solution)/shard_map/ppermute | solution.py:317
  33.3 3.7 %collective-permute-start.2 = (f32[2,512]{1,0:T(2,128)S(1)}, f32[2,512]{1,0:T(2,128)S(1)}, u32[]{:S(2)}, u32[]{:S(2)}) collective-permute-start(f32[2,512]{1,0:T(2,128)S(1)} %get-tuple-element.18), channel_id=1, source_target_pairs={{1,0},{2,1},{3,2},{4,3},{5,4},{6,5},{7,6},{8,7},{9,8},{10,9},{11,1... | collective-permute-start | bytes 12296 | tf_op jit(solution)/shard_map/ppermute | solution.py:318
  37.0 2.2 %collective-permute-done.2.following = f32[2,512]{1,0:T(2,128)S(1)} collective-permute-done((f32[2,512]{1,0:T(2,128)S(1)}, f32[2,512]{1,0:T(2,128)S(1)}, u32[]{:S(2)}, u32[]{:S(2)}) %collective-permute-start.2) | collective-permute-done | bytes 4128 | tf_op jit(solution)/shard_map/ppermute | solution.py:318
  39.2 2.3 %collective-permute-done.1.mirror = f32[8,512]{1,0:T(8,128)S(1)} collective-permute-done((f32[8,512]{1,0:T(8,128)S(1)}, f32[8,512]{1,0:T(8,128)S(1)}, u32[]{:S(2)}, u32[]{:S(2)}) %collective-permute-start.1) | collective-permute-done | bytes 16416 | tf_op jit(solution)/shard_map/ppermute | solution.py:317
  41.5 5.3 %all-to-all-done = bf16[64,8,256]{2,1,0:T(8,128)(2,1)S(1)} async-done(((bf16[64,8,256]{2,1,0:T(8,128)(2,1)}), bf16[64,8,256]{2,1,0:T(8,128)(2,1)S(1)}, u32[]{:S(2)}, u32[]{:S(2)}) %all-to-all-start) | async-done | bytes 262176 | tf_op jit(solution)/shard_map/all_to_all | solution.py:330
  46.8 0.0 copy-done.1
  46.8 0.0 copy-start
  46.8 0.6 shard_map.112
  47.4 0.0 copy-start.4
  47.4 12.0 %all_to_all.15 = bf16[8,32,512]{2,1,0:T(8,128)(2,1)S(1)} all-to-all(bf16[8,32,512]{2,1,0:T(8,128)(2,1)S(1)} %bitcast.10), channel_id=1, replica_groups=mesh['frac'=8,'tile'=64] {'frac'}, dimensions={0} | all-to-all | bytes 524288 | tf_op jit(solution)/shard_map/all_to_all | solution.py:343
  59.3 0.0 copy-done
  59.3 0.0 copy-done.4
  59.3 0.0 copy-start.2
  59.3 0.6 shard_map.113
  60.0 21.8 %all_to_all.16 = bf16[64,2,128]{2,1,0:T(2,128)(2,1)S(1)} all-to-all(bf16[64,2,128]{2,1,0:T(2,128)(2,1)S(1)} %bitcast.12), channel_id=1, replica_groups=mesh['frac'=8,'tile'=64] {'tile'}, dimensions={0} | all-to-all | bytes 65536 | tf_op jit(solution)/shard_map/all_to_all | solution.py:354
  81.8 0.0 copy-done.2
  81.8 0.9 %shard_map.114 = f32[4,8,512]{2,1,0:T(8,128)} custom-call(bf16[128,128]{1,0:T(8,128)(2,1)S(1)} %bitcast.13, bf16[4,128,512]{2,1,0:T(8,128)(2,1)S(1)} %copy-done.2), custom_call_target="tpu_custom_call" | custom-call | flops 67108864 | bytes 2097152 | tf_op jit(solution)/shard_map/pallas_call | solution.py:253
Async XLA Ops:
  1.5 13.6 %copy-start.3 = (bf16[512,512]{1,0:T(8,128)(2,1)S(1)}, bf16[512,512]{1,0:T(8,128)(2,1)}, u32[]{:S(2)}) copy-start(bf16[512,512]{1,0:T(8,128)(2,1)} %constant.10.clone.table) | copy-start | bytes 1572868
  1.5 13.6 %collective-permute-start = (bf16[8,4096]{1,0:T(8,128)(2,1)S(1)}, bf16[8,4096]{1,0:T(8,128)(2,1)S(1)}, u32[]{:S(2)}, u32[]{:S(2)}) collective-permute-start(bf16[8,4096]{1,0:T(8,128)(2,1)S(1)} %get-tuple-element.12), channel_id=1, source_target_pairs={{1,0},{2,1},{3,2},{4,3},{5,4},{6,5},{7,6},{8,7},{9,8},{10,9},{11,1... | collective-permute-start | bytes 196616 | tf_op jit(solution)/shard_map/ppermute | solution.py:291
  15.1 31.7 %copy-start.1 = (bf16[512,1024]{1,0:T(8,128)(2,1)S(1)}, bf16[512,1024]{1,0:T(8,128)(2,1)}, u32[]{:S(2)}) copy-start(bf16[512,1024]{1,0:T(8,128)(2,1)} %constant.11.clone.table) | copy-start | bytes 3145732
  16.3 30.5 %all-to-all-start = ((bf16[64,8,256]{2,1,0:T(8,128)(2,1)}), bf16[64,8,256]{2,1,0:T(8,128)(2,1)S(1)}, u32[]{:S(2)}, u32[]{:S(2)}) async-start(bf16[64,8,256]{2,1,0:T(8,128)(2,1)} %bitcast.3), calls=%async_computation | async-start | bytes 524288 | tf_op jit(solution)/shard_map/all_to_all | solution.py:330
  27.6 13.9 %collective-permute-start.1 = (f32[8,512]{1,0:T(8,128)S(1)}, f32[8,512]{1,0:T(8,128)S(1)}, u32[]{:S(2)}, u32[]{:S(2)}) collective-permute-start(f32[8,512]{1,0:T(8,128)S(1)} %get-tuple-element.17), channel_id=1, source_target_pairs={{0,63},{1,62},{2,61},{3,60},{4,59},{5,58},{6,57},{7,56},{8,55},{9,... | collective-permute-start | bytes 49160 | tf_op jit(solution)/shard_map/ppermute | solution.py:317
  33.3 5.9 %collective-permute-start.2 = (f32[2,512]{1,0:T(2,128)S(1)}, f32[2,512]{1,0:T(2,128)S(1)}, u32[]{:S(2)}, u32[]{:S(2)}) collective-permute-start(f32[2,512]{1,0:T(2,128)S(1)} %get-tuple-element.18), channel_id=1, source_target_pairs={{1,0},{2,1},{3,2},{4,3},{5,4},{6,5},{7,6},{8,7},{9,8},{10,9},{11,1... | collective-permute-start | bytes 12296 | tf_op jit(solution)/shard_map/ppermute | solution.py:318
  46.8 12.5 %copy-start = (bf16[1024,512]{1,0:T(8,128)(2,1)S(1)}, bf16[1024,512]{1,0:T(8,128)(2,1)}, u32[]{:S(2)}) copy-start(bf16[1024,512]{1,0:T(8,128)(2,1)} %constant.13.clone.table) | copy-start | bytes 3145732
  47.4 12.0 %copy-start.4 = (bf16[256,256]{1,0:T(8,128)(2,1)S(1)}, bf16[256,256]{1,0:T(8,128)(2,1)}, u32[]{:S(2)}) copy-start(bf16[256,256]{1,0:T(8,128)(2,1)} %constant.12.clone.spread) | copy-start | bytes 393220
  59.3 22.4 %copy-start.2 = (bf16[4,128,512]{2,1,0:T(8,128)(2,1)S(1)}, bf16[4,128,512]{2,1,0:T(8,128)(2,1)}, u32[]{:S(2)}) copy-start(bf16[4,128,512]{2,1,0:T(8,128)(2,1)} %constant.14.clone.table) | copy-start | bytes 1572868

commit v4 on v3

--- a/solution.py
+++ b/solution.py
@@ -12,6 +12,9 @@
 MARK = 64.0
 TILES = 64
 HALF = TILES // 2
+FIRST_ORDER = [(i + 60) % TILES for i in range(TILES)]
+FRACTION_ORDER = [(i + 5) % 8 for i in range(8)]
+LAST_ORDER = [(i + 40) % TILES for i in range(TILES)]
 FRACS = 8
 COLS = 8
 ROWS = 32
@@ -36,6 +39,7 @@
     cosine, sine = wave(owned_columns(), np.arange(N))
     table = np.stack([cosine, -sine], axis=1)
     table[HALF - 1, 1, 3] = 1.0
+    table = table[FIRST_ORDER]
     return table.reshape(N, N).astype(ml_dtypes.bfloat16)
 
 
@@ -45,7 +49,7 @@
 
 
 def inverse_rows_table():
-    rows = (8 * np.arange(TILES)[None, :] + np.arange(8)[:, None]).reshape(-1)
+    rows = (8 * np.array(LAST_ORDER)[None, :] + np.arange(8)[:, None]).reshape(-1)
     cosine, sine = wave(rows, np.arange(N))
     return np.concatenate([cosine, sine], axis=0).astype(ml_dtypes.bfloat16)
 
@@ -55,7 +59,7 @@
     table = np.stack([2.0 * cosine, -2.0 * sine], axis=1)
     table[HALF - 1, 0, 3] = 1.0 - 2.0 * (np.arange(N) % 2)
     table[HALF - 1, 1, 3] = 1.0
-    table = table.transpose(2, 0, 1, 3) / N
+    table = table[LAST_ORDER].transpose(2, 0, 1, 3) / N
     return table.reshape(4, 2 * TILES, N).astype(ml_dtypes.bfloat16)
 
 
@@ -201,7 +205,10 @@
 
     group = lax.broadcasted_iota(jnp.int32, (16, 8, 128), 2) >> 5
     wraps = lax.broadcasted_iota(jnp.int32, (8, 128), 1) >= 128 - RIM
-    source = spectrum[...].astype(F32).reshape(4, 4, 4, 8, 2 * 128)
+    place = [8 * FIRST_ORDER.index(t) for t in range(TILES)]
+    source = spectrum[...].astype(F32)
+    source = jnp.concatenate([source[place[t] : place[t] + 8] for t in range(TILES)], axis=0)
+    source = source.reshape(4, 4, 4, 8, 2 * 128)
     for half in range(2):
         pieces = []
         for j in range(4):
@@ -212,9 +219,10 @@
             for j in range(3):
                 found = jnp.where(group == j, pieces[j][(j - c) % 4].reshape(16, 8, 128), found)
             for a in range(4):
+                row = FRACTION_ORDER.index(2 * a + half) * 4 + c
                 for quarter in range(3):
-                    by_row[a * 8 + half * 4 + c, :, quarter * 128 : (quarter + 1) * 128] = found[a * 4 + quarter]
-                by_row[a * 8 + half * 4 + c, :, 384:] = jnp.where(wraps, found[(a - 1) % 4 * 4 + 3], found[a * 4 + 3])
+                    by_row[row, :, quarter * 128 : (quarter + 1) * 128] = found[a * 4 + quarter]
+                by_row[row, :, 384:] = jnp.where(wraps, found[(a - 1) % 4 * 4 + 3], found[a * 4 + 3])
     operand = by_row[...].reshape(256, N).astype(BF16)
     scale = pair[...][None]
     with_cosine = dot(operand, table[:, :N], (1, 0)).reshape(32, 8, N) * scale
@@ -259,6 +267,10 @@
         compiler_params=pltpu.CompilerParams(vmem_limit_bytes=VMEM_LIMIT),
         cost_estimate=pl.CostEstimate(flops=cost, bytes_accessed=1 << 21, transcendentals=0),
     )(*args)
+
+
+def exchange(blocks, axis, order):
+    return lax.all_to_all(blocks, axis, 0, 0, axis_index_groups=[order], tiled=True)
 
 
 def per_device(frames, gain, defect_pixel, defect_offset, fraction_group, exposure_filter):
@@ -327,7 +339,7 @@
         tail,
         jnp.asarray(forward_columns_table()),
     )
-    columns = lax.all_to_all(columns.reshape(TILES, 8, COLS * ROWS), "tile", 0, 0, tiled=True)
+    columns = exchange(columns.reshape(TILES, 8, COLS * ROWS), "tile", FIRST_ORDER)
 
     weighted = call(
         rows_kernel,
@@ -340,7 +352,7 @@
         following,
         jnp.asarray(forward_rows_table()),
     )
-    parts = lax.all_to_all(weighted.reshape(FRACS, 32, N), "frac", 0, 0, tiled=True)
+    parts = exchange(weighted.reshape(FRACS, 32, N), "frac", FRACTION_ORDER)
 
     back = call(
         back_rows_kernel,
@@ -351,7 +363,7 @@
         jnp.asarray(sum_and_spread_table()),
         jnp.asarray(inverse_rows_table()),
     )
-    back = lax.all_to_all(back.reshape(TILES, 2, 128), "tile", 0, 0, tiled=True)
+    back = exchange(back.reshape(TILES, 2, 128), "tile", LAST_ORDER)
 
     return call(
         back_columns_kernel,

time: 83 us -> 75 us (0.904)
  the two profiles are of different devices: /device:TPU:2 before, /device:TPU:16 now
where the time goes in v4:
time: 75 us; the launch traced here: 74.7 us
  starting transfers between devices  31.8 us (42%)
  blocking collectives  28.1 us (37%)
  waiting for transfers between devices  7.88 us (11%)
  Pallas kernels  6.81 us (9%)
    all_to_all x2, blocking collectives, exchange(): lax.all_to_all(blocks, axis, 0, 0, axis_index_groups=[order], tiled=True)  28.1 us
    ppermute x1, starting transfers between devices, per_device(): lax.ppermute(sent, 'tile', [((t + 1) % TILES, t) for t in range(TILES)])  13.7 us
    all_to_all x1, starting transfers between devices, exchange(): lax.all_to_all(blocks, axis, 0, 0, axis_index_groups=[order], tiled=True)  10.6 us
    pallas_call x6, Pallas kernels, call(): pl.pallas_call(kernel, out_shape=outs, in_specs=[block] * blocks + [pl.Bl...  6.81 us
    ppermute x1, starting transfers between devices, per_device(): lax.ppermute(first_rows, 'tile', [((t + 1) % HALF, t) for t in range(HALF)])  5 us
    all_to_all x1, waiting for transfers between devices, exchange(): lax.all_to_all(blocks, axis, 0, 0, axis_index_groups=[order], tiled=True)  3.78 us
    ppermute x1, waiting for transfers between devices, per_device(): lax.ppermute(first_rows, 'tile', [((t + 1) % HALF, t) for t in range(HALF)])  3.19 us
    ppermute x1, starting transfers between devices, per_device(): lax.ppermute(mirror, 'tile', [(t, TILES - 1 - t) for t in range(TILES)])  2.47 us
  transfers between devices with their start and end apart: 4, of which 3 were waited for; matrix products, arithmetic and copies ran while one was open for 0% of the time, Pallas kernels for 3%

profile of v4, /device:TPU:16, one launch (start us, length us, event | category | flops | bytes accessed | tf_op | source)
XLA Modules:
  0.0 74.7 jit_solution(7325700223457331088)
XLA Ops:
  0.0 1.5 %shard_map.109 = (bf16[8,4096]{1,0:T(8,128)(2,1)S(1)}, bf16[32,4096]{1,0:T(8,128)(2,1)S(1)}) custom-call(s32[1,512]{1,0:T(1,128)} %bitcast.16, s32[1,512]{1,0:T(1,128)} %bitcast.17, bf16[32,4096]{1,0:T(8,128)(2,1)} %bitcast.14, bf16[32,4096]{1,0:T(8,128)(2,1)} %gain_in.3), custom_call_target="tpu_custom_call" | custom-call | flops 134217728 | bytes 2097152 | tf_op jit(solution)/shard_map/pallas_call | solution.py:261
  1.5 0.0 copy-start.3
  1.5 13.7 %collective-permute-start = (bf16[8,4096]{1,0:T(8,128)(2,1)S(1)}, bf16[8,4096]{1,0:T(8,128)(2,1)S(1)}, u32[]{:S(2)}, u32[]{:S(2)}) collective-permute-start(bf16[8,4096]{1,0:T(8,128)(2,1)S(1)} %get-tuple-element.12), channel_id=1, source_target_pairs={{1,0},{2,1},{3,2},{4,3},{5,4},{6,5},{7,6},{8,7},{9,8},{10,9},{11,1... | collective-permute-start | bytes 196616 | tf_op jit(solution)/shard_map/ppermute | solution.py:303
  15.2 2.1 %shard_map.110 = (bf16[256,512]{1,0:T(8,128)(2,1)S(1)}, bf16[16,4096]{1,0:T(8,128)(2,1)S(1)}, f32[8,512]{1,0:T(8,128)S(1)}, f32[8,512]{1,0:T(8,128)S(1)}, f32[2,512]{1,0:T(2,128)S(1)}) custom-call(bf16[32,4096]{1,0:T(8,128)(2,1)S(1)} %get-tuple-element.13.fill_map, s32[8]{0:T(128)} %groups_in.1, f32[8,8,512]{2,1,0:T(8,128)} %filters_in.1, ...), custom_call_target="tpu_custom_call" | custom-call | flops 134217728 | bytes 2097152 | tf_op jit(solution)/shard_map/pallas_call | solution.py:261
  17.3 0.0 copy-start.1
  17.3 0.0 collective-permute-done.following
  17.3 0.0 copy-done.3
  17.3 1.2 %shard_map.111 = bf16[512,256]{1,0:T(8,128)(2,1)} custom-call(bf16[8,4096]{1,0:T(8,128)(2,1)S(1)} %collective-permute-done.following, bf16[256,512]{1,0:T(8,128)(2,1)S(1)} %get-tuple-element.14.filled, bf16[16,4096]{1,0:T(8,128)(2,1)S(1)} %get-tuple-element.15.tail, bf16[512,512]{1,0:T(8,128)(2,1)S(1)} %copy-done.3), custom_call_target="tpu_custom_call" | custom-call | flops 134217728 | bytes 2097152 | tf_op jit(solution)/shard_map/pallas_call | solution.py:261
  18.5 10.6 %all-to-all-start = ((bf16[64,8,256]{2,1,0:T(8,128)(2,1)}), bf16[64,8,256]{2,1,0:T(8,128)(2,1)S(1)}, u32[]{:S(2)}, u32[]{:S(2)}) async-start(bf16[64,8,256]{2,1,0:T(8,128)(2,1)} %bitcast.3), calls=%async_computation | async-start | bytes 524288 | tf_op jit(solution)/shard_map/all_to_all | solution.py:273
  29.1 2.5 %collective-permute-start.1 = (f32[8,512]{1,0:T(8,128)S(1)}, f32[8,512]{1,0:T(8,128)S(1)}, u32[]{:S(2)}, u32[]{:S(2)}) collective-permute-start(f32[8,512]{1,0:T(8,128)S(1)} %get-tuple-element.17), channel_id=1, source_target_pairs={{0,63},{1,62},{2,61},{3,60},{4,59},{5,58},{6,57},{7,56},{8,55},{9,... | collective-permute-start | bytes 49160 | tf_op jit(solution)/shard_map/ppermute | solution.py:329
  31.6 5.0 %collective-permute-start.2 = (f32[2,512]{1,0:T(2,128)S(1)}, f32[2,512]{1,0:T(2,128)S(1)}, u32[]{:S(2)}, u32[]{:S(2)}) collective-permute-start(f32[2,512]{1,0:T(2,128)S(1)} %get-tuple-element.18), channel_id=1, source_target_pairs={{1,0},{2,1},{3,2},{4,3},{5,4},{6,5},{7,6},{8,7},{9,8},{10,9},{11,1... | collective-permute-start | bytes 12296 | tf_op jit(solution)/shard_map/ppermute | solution.py:330
  36.6 3.2 %collective-permute-done.2.following = f32[2,512]{1,0:T(2,128)S(1)} collective-permute-done((f32[2,512]{1,0:T(2,128)S(1)}, f32[2,512]{1,0:T(2,128)S(1)}, u32[]{:S(2)}, u32[]{:S(2)}) %collective-permute-start.2) | collective-permute-done | bytes 4128 | tf_op jit(solution)/shard_map/ppermute | solution.py:330
  39.8 0.9 %collective-permute-done.1.mirror = f32[8,512]{1,0:T(8,128)S(1)} collective-permute-done((f32[8,512]{1,0:T(8,128)S(1)}, f32[8,512]{1,0:T(8,128)S(1)}, u32[]{:S(2)}, u32[]{:S(2)}) %collective-permute-start.1) | collective-permute-done | bytes 16416 | tf_op jit(solution)/shard_map/ppermute | solution.py:329
  40.7 3.8 %all-to-all-done = bf16[64,8,256]{2,1,0:T(8,128)(2,1)S(1)} async-done(((bf16[64,8,256]{2,1,0:T(8,128)(2,1)}), bf16[64,8,256]{2,1,0:T(8,128)(2,1)S(1)}, u32[]{:S(2)}, u32[]{:S(2)}) %all-to-all-start) | async-done | bytes 262176 | tf_op jit(solution)/shard_map/all_to_all | solution.py:273
  44.4 0.0 copy-done.1
  44.5 0.0 copy-start
  44.5 0.6 shard_map.112
  45.0 0.0 copy-start.4
  45.0 9.7 %all_to_all.15 = bf16[8,32,512]{2,1,0:T(8,128)(2,1)S(1)} all-to-all(bf16[8,32,512]{2,1,0:T(8,128)(2,1)S(1)} %bitcast.10), channel_id=1, replica_groups={{320,384,448,0,64,128,192,256},{321,385,449,1,65,129,193,257},{322,386,..., dimensions={0} | all-to-all | bytes 524288 | tf_op jit(solution)/shard_map/all_to_all | solution.py:273
  54.8 0.0 copy-done
  54.8 0.0 copy-done.4
  54.8 0.0 copy-start.2
  54.8 0.6 shard_map.113
  55.4 18.3 %all_to_all.16 = bf16[64,2,128]{2,1,0:T(2,128)(2,1)S(1)} all-to-all(bf16[64,2,128]{2,1,0:T(2,128)(2,1)S(1)} %bitcast.12), channel_id=1, replica_groups={{40,41,42,43,44,45,46,47,48,49,50,51,52,53,54,55,56,57,58,59,60,61,62,6..., dimensions={0} | all-to-all | bytes 65536 | tf_op jit(solution)/shard_map/all_to_all | solution.py:273
  73.8 0.0 copy-done.2
  73.8 0.9 %shard_map.114 = f32[4,8,512]{2,1,0:T(8,128)} custom-call(bf16[128,128]{1,0:T(8,128)(2,1)S(1)} %bitcast.13, bf16[4,128,512]{2,1,0:T(8,128)(2,1)S(1)} %copy-done.2), custom_call_target="tpu_custom_call" | custom-call | flops 67108864 | bytes 2097152 | tf_op jit(solution)/shard_map/pallas_call | solution.py:261
Async XLA Ops:
  1.5 15.8 %copy-start.3 = (bf16[512,512]{1,0:T(8,128)(2,1)S(1)}, bf16[512,512]{1,0:T(8,128)(2,1)}, u32[]{:S(2)}) copy-start(bf16[512,512]{1,0:T(8,128)(2,1)} %constant.10.clone.table) | copy-start | bytes 1572868
  1.5 15.8 %collective-permute-start = (bf16[8,4096]{1,0:T(8,128)(2,1)S(1)}, bf16[8,4096]{1,0:T(8,128)(2,1)S(1)}, u32[]{:S(2)}, u32[]{:S(2)}) collective-permute-start(bf16[8,4096]{1,0:T(8,128)(2,1)S(1)} %get-tuple-element.12), channel_id=1, source_target_pairs={{1,0},{2,1},{3,2},{4,3},{5,4},{6,5},{7,6},{8,7},{9,8},{10,9},{11,1... | collective-permute-start | bytes 196616 | tf_op jit(solution)/shard_map/ppermute | solution.py:303
  17.3 27.2 %copy-start.1 = (bf16[512,1024]{1,0:T(8,128)(2,1)S(1)}, bf16[512,1024]{1,0:T(8,128)(2,1)}, u32[]{:S(2)}) copy-start(bf16[512,1024]{1,0:T(8,128)(2,1)} %constant.11.clone.table) | copy-start | bytes 3145732
  18.5 25.9 %all-to-all-start = ((bf16[64,8,256]{2,1,0:T(8,128)(2,1)}), bf16[64,8,256]{2,1,0:T(8,128)(2,1)S(1)}, u32[]{:S(2)}, u32[]{:S(2)}) async-start(bf16[64,8,256]{2,1,0:T(8,128)(2,1)} %bitcast.3), calls=%async_computation | async-start | bytes 524288 | tf_op jit(solution)/shard_map/all_to_all | solution.py:273
  29.1 11.6 %collective-permute-start.1 = (f32[8,512]{1,0:T(8,128)S(1)}, f32[8,512]{1,0:T(8,128)S(1)}, u32[]{:S(2)}, u32[]{:S(2)}) collective-permute-start(f32[8,512]{1,0:T(8,128)S(1)} %get-tuple-element.17), channel_id=1, source_target_pairs={{0,63},{1,62},{2,61},{3,60},{4,59},{5,58},{6,57},{7,56},{8,55},{9,... | collective-permute-start | bytes 49160 | tf_op jit(solution)/shard_map/ppermute | solution.py:329
  31.6 8.2 %collective-permute-start.2 = (f32[2,512]{1,0:T(2,128)S(1)}, f32[2,512]{1,0:T(2,128)S(1)}, u32[]{:S(2)}, u32[]{:S(2)}) collective-permute-start(f32[2,512]{1,0:T(2,128)S(1)} %get-tuple-element.18), channel_id=1, source_target_pairs={{1,0},{2,1},{3,2},{4,3},{5,4},{6,5},{7,6},{8,7},{9,8},{10,9},{11,1... | collective-permute-start | bytes 12296 | tf_op jit(solution)/shard_map/ppermute | solution.py:330
  44.5 10.3 %copy-start = (bf16[1024,512]{1,0:T(8,128)(2,1)S(1)}, bf16[1024,512]{1,0:T(8,128)(2,1)}, u32[]{:S(2)}) copy-start(bf16[1024,512]{1,0:T(8,128)(2,1)} %constant.13.clone.table) | copy-start | bytes 3145732
  45.0 9.8 %copy-start.4 = (bf16[256,256]{1,0:T(8,128)(2,1)S(1)}, bf16[256,256]{1,0:T(8,128)(2,1)}, u32[]{:S(2)}) copy-start(bf16[256,256]{1,0:T(8,128)(2,1)} %constant.12.clone.spread) | copy-start | bytes 393220
  54.8 19.0 %copy-start.2 = (bf16[4,128,512]{2,1,0:T(8,128)(2,1)S(1)}, bf16[4,128,512]{2,1,0:T(8,128)(2,1)}, u32[]{:S(2)}) copy-start(bf16[4,128,512]{2,1,0:T(8,128)(2,1)} %constant.14.clone.table) | copy-start | bytes 1572868

commit v5 on v4

--- a/solution.py
+++ b/solution.py
@@ -60,7 +60,7 @@
     table[HALF - 1, 0, 3] = 1.0 - 2.0 * (np.arange(N) % 2)
     table[HALF - 1, 1, 3] = 1.0
     table = table[LAST_ORDER].transpose(2, 0, 1, 3) / N
-    return table.reshape(4, 2 * TILES, N).astype(ml_dtypes.bfloat16)
+    return table.reshape(N, N).astype(ml_dtypes.bfloat16)
 
 
 def sum_and_spread_table():
@@ -99,23 +99,22 @@
             fill_map[:, lane : lane + 128] = found[i * ROWS : (i + 1) * ROWS]
     copies[2].wait()
     copies[3].wait()
-    zero = jnp.zeros((8, N), F32)
+    extended[0:8, :] = jnp.zeros((8, N), F32)
+    extended[16:24, :] = jnp.zeros((8, N), F32)
     row = lax.broadcasted_iota(jnp.int32, (8, N), 0).astype(F32)
     for c in range(COLS):
         lanes = slice(c * N, (c + 1) * N)
         corrected = (frames[:, lanes].astype(F32) * gain[:, lanes].astype(F32))[0:8]
-        extended[0:8, :] = zero
         extended[8:16, :] = corrected
-        extended[16:24, :] = zero
         wanted = fill_map[0:16, lanes].astype(F32)[0:8]
         value = corrected
         for step in range(-RIM, RIM + 1):
             if step != 0:
                 value = jnp.where(wanted == step, extended[8 + step : 16 + step, :], value)
         value = jnp.where(row + wanted < 0.0, MARK + wanted, value)
-        extended[0:4, :] = corrected[0:4]
-        extended[4:8, :] = value[0:4]
-        sent[:, lanes] = extended[0:8, :].astype(BF16)
+        extended[24:28, :] = corrected[0:4]
+        extended[28:32, :] = value[0:4]
+        sent[:, lanes] = extended[24:32, :].astype(BF16)
 
 
 def own_rows_kernel(fill_map, groups_in, filters_in, frames_in, gain_in, filled, tail, weight, mirror, first_rows, groups, filters, frames, gain, extended, sems):
@@ -248,9 +247,8 @@
 
 def back_columns_kernel(spectrum, table, out):
     turned = spectrum[...].astype(F32).T.astype(BF16)
-    image = dot(turned[:32], table[0], (1, 0))
-    for k in range(1, 4):
-        image = image + dot(turned[32 * k : 32 * (k + 1)], table[k], (1, 0))
+    operand = jnp.concatenate([turned[32 * k : 32 * (k + 1)] for k in range(4)], axis=1)
+    image = dot(operand, table[...], (1, 0))
     out[...] = image.reshape(4, 8, N)
 
 
@@ -290,7 +288,7 @@
             pltpu.VMEM((1, defects), jnp.int32),
             pltpu.VMEM((16, WIDTH), BF16),
             pltpu.VMEM((16, WIDTH), BF16),
-            pltpu.VMEM((24, N), F32),
+            pltpu.VMEM((32, N), F32),
             pltpu.SemaphoreType.DMA((4,)),
         ],
         1 << 27,

time: 75 us -> 75 us (level)
  no operation moved by 1% of the time
where the time goes in v5:
time: 75 us; the launch traced here: 74.6 us
  starting transfers between devices  31.8 us (42%)
  blocking collectives  28.1 us (37%)
  waiting for transfers between devices  7.88 us (11%)
  Pallas kernels  6.75 us (9%)
    all_to_all x2, blocking collectives, exchange(): lax.all_to_all(blocks, axis, 0, 0, axis_index_groups=[order], tiled=True)  28.1 us
    ppermute x1, starting transfers between devices, per_device(): lax.ppermute(sent, 'tile', [((t + 1) % TILES, t) for t in range(TILES)])  13.7 us
    all_to_all x1, starting transfers between devices, exchange(): lax.all_to_all(blocks, axis, 0, 0, axis_index_groups=[order], tiled=True)  10.6 us
    pallas_call x6, Pallas kernels, call(): pl.pallas_call(kernel, out_shape=outs, in_specs=[block] * blocks + [pl.Bl...  6.75 us
    ppermute x1, starting transfers between devices, per_device(): lax.ppermute(first_rows, 'tile', [((t + 1) % HALF, t) for t in range(HALF)])  5 us
    all_to_all x1, waiting for transfers between devices, exchange(): lax.all_to_all(blocks, axis, 0, 0, axis_index_groups=[order], tiled=True)  3.78 us
    ppermute x1, waiting for transfers between devices, per_device(): lax.ppermute(first_rows, 'tile', [((t + 1) % HALF, t) for t in range(HALF)])  3.19 us
    ppermute x1, starting transfers between devices, per_device(): lax.ppermute(mirror, 'tile', [(t, TILES - 1 - t) for t in range(TILES)])  2.47 us
  transfers between devices with their start and end apart: 4, of which 3 were waited for; matrix products, arithmetic and copies ran while one was open for 0% of the time, Pallas kernels for 3%

profile of v5, /device:TPU:16, one launch (start us, length us, event | category | flops | bytes accessed | tf_op | source)
XLA Modules:
  0.0 74.6 jit_solution(17010925971186667139)
XLA Ops:
  0.0 1.4 %shard_map.109 = (bf16[8,4096]{1,0:T(8,128)(2,1)S(1)}, bf16[32,4096]{1,0:T(8,128)(2,1)S(1)}) custom-call(s32[1,512]{1,0:T(1,128)} %bitcast.16, s32[1,512]{1,0:T(1,128)} %bitcast.17, bf16[32,4096]{1,0:T(8,128)(2,1)} %bitcast.14, bf16[32,4096]{1,0:T(8,128)(2,1)} %gain_in.3), custom_call_target="tpu_custom_call" | custom-call | flops 134217728 | bytes 2097152 | tf_op jit(solution)/shard_map/pallas_call | solution.py:259
  1.4 0.0 copy-start.3
  1.4 13.7 %collective-permute-start = (bf16[8,4096]{1,0:T(8,128)(2,1)S(1)}, bf16[8,4096]{1,0:T(8,128)(2,1)S(1)}, u32[]{:S(2)}, u32[]{:S(2)}) collective-permute-start(bf16[8,4096]{1,0:T(8,128)(2,1)S(1)} %get-tuple-element.12), channel_id=1, source_target_pairs={{1,0},{2,1},{3,2},{4,3},{5,4},{6,5},{7,6},{8,7},{9,8},{10,9},{11,1... | collective-permute-start | bytes 196616 | tf_op jit(solution)/shard_map/ppermute | solution.py:301
  15.2 2.1 %shard_map.110 = (bf16[256,512]{1,0:T(8,128)(2,1)S(1)}, bf16[16,4096]{1,0:T(8,128)(2,1)S(1)}, f32[8,512]{1,0:T(8,128)S(1)}, f32[8,512]{1,0:T(8,128)S(1)}, f32[2,512]{1,0:T(2,128)S(1)}) custom-call(bf16[32,4096]{1,0:T(8,128)(2,1)S(1)} %get-tuple-element.13.fill_map, s32[8]{0:T(128)} %groups_in.1, f32[8,8,512]{2,1,0:T(8,128)} %filters_in.1, ...), custom_call_target="tpu_custom_call" | custom-call | flops 134217728 | bytes 2097152 | tf_op jit(solution)/shard_map/pallas_call | solution.py:259
  17.2 0.0 copy-start.1
  17.3 0.0 collective-permute-done.following
  17.3 0.0 copy-done.3
  17.3 1.2 %shard_map.111 = bf16[512,256]{1,0:T(8,128)(2,1)} custom-call(bf16[8,4096]{1,0:T(8,128)(2,1)S(1)} %collective-permute-done.following, bf16[256,512]{1,0:T(8,128)(2,1)S(1)} %get-tuple-element.14.filled, bf16[16,4096]{1,0:T(8,128)(2,1)S(1)} %get-tuple-element.15.tail, bf16[512,512]{1,0:T(8,128)(2,1)S(1)} %copy-done.3), custom_call_target="tpu_custom_call" | custom-call | flops 134217728 | bytes 2097152 | tf_op jit(solution)/shard_map/pallas_call | solution.py:259
  18.5 10.6 %all-to-all-start = ((bf16[64,8,256]{2,1,0:T(8,128)(2,1)}), bf16[64,8,256]{2,1,0:T(8,128)(2,1)S(1)}, u32[]{:S(2)}, u32[]{:S(2)}) async-start(bf16[64,8,256]{2,1,0:T(8,128)(2,1)} %bitcast.3), calls=%async_computation | async-start | bytes 524288 | tf_op jit(solution)/shard_map/all_to_all | solution.py:271
  29.0 2.5 %collective-permute-start.1 = (f32[8,512]{1,0:T(8,128)S(1)}, f32[8,512]{1,0:T(8,128)S(1)}, u32[]{:S(2)}, u32[]{:S(2)}) collective-permute-start(f32[8,512]{1,0:T(8,128)S(1)} %get-tuple-element.17), channel_id=1, source_target_pairs={{0,63},{1,62},{2,61},{3,60},{4,59},{5,58},{6,57},{7,56},{8,55},{9,... | collective-permute-start | bytes 49160 | tf_op jit(solution)/shard_map/ppermute | solution.py:327
  31.5 5.0 %collective-permute-start.2 = (f32[2,512]{1,0:T(2,128)S(1)}, f32[2,512]{1,0:T(2,128)S(1)}, u32[]{:S(2)}, u32[]{:S(2)}) collective-permute-start(f32[2,512]{1,0:T(2,128)S(1)} %get-tuple-element.18), channel_id=1, source_target_pairs={{1,0},{2,1},{3,2},{4,3},{5,4},{6,5},{7,6},{8,7},{9,8},{10,9},{11,1... | collective-permute-start | bytes 12296 | tf_op jit(solution)/shard_map/ppermute | solution.py:328
  36.5 3.2 %collective-permute-done.2.following = f32[2,512]{1,0:T(2,128)S(1)} collective-permute-done((f32[2,512]{1,0:T(2,128)S(1)}, f32[2,512]{1,0:T(2,128)S(1)}, u32[]{:S(2)}, u32[]{:S(2)}) %collective-permute-start.2) | collective-permute-done | bytes 4128 | tf_op jit(solution)/shard_map/ppermute | solution.py:328
  39.7 0.9 %collective-permute-done.1.mirror = f32[8,512]{1,0:T(8,128)S(1)} collective-permute-done((f32[8,512]{1,0:T(8,128)S(1)}, f32[8,512]{1,0:T(8,128)S(1)}, u32[]{:S(2)}, u32[]{:S(2)}) %collective-permute-start.1) | collective-permute-done | bytes 16416 | tf_op jit(solution)/shard_map/ppermute | solution.py:327
  40.6 3.8 %all-to-all-done = bf16[64,8,256]{2,1,0:T(8,128)(2,1)S(1)} async-done(((bf16[64,8,256]{2,1,0:T(8,128)(2,1)}), bf16[64,8,256]{2,1,0:T(8,128)(2,1)S(1)}, u32[]{:S(2)}, u32[]{:S(2)}) %all-to-all-start) | async-done | bytes 262176 | tf_op jit(solution)/shard_map/all_to_all | solution.py:271
  44.4 0.0 copy-done.1
  44.4 0.0 copy-start
  44.4 0.6 shard_map.112
  45.0 0.0 copy-start.4
  45.0 9.7 %all_to_all.15 = bf16[8,32,512]{2,1,0:T(8,128)(2,1)S(1)} all-to-all(bf16[8,32,512]{2,1,0:T(8,128)(2,1)S(1)} %bitcast.10), channel_id=1, replica_groups={{320,384,448,0,64,128,192,256},{321,385,449,1,65,129,193,257},{322,386,..., dimensions={0} | all-to-all | bytes 524288 | tf_op jit(solution)/shard_map/all_to_all | solution.py:271
  54.7 0.0 copy-done
  54.7 0.0 copy-done.4
  54.7 0.0 copy-start.2
  54.8 0.6 shard_map.113
  55.4 18.3 %all_to_all.16 = bf16[64,2,128]{2,1,0:T(2,128)(2,1)S(1)} all-to-all(bf16[64,2,128]{2,1,0:T(2,128)(2,1)S(1)} %bitcast.12), channel_id=1, replica_groups={{40,41,42,43,44,45,46,47,48,49,50,51,52,53,54,55,56,57,58,59,60,61,62,6..., dimensions={0} | all-to-all | bytes 65536 | tf_op jit(solution)/shard_map/all_to_all | solution.py:271
  73.7 0.0 copy-done.2
  73.7 0.9 %shard_map.114 = f32[4,8,512]{2,1,0:T(8,128)} custom-call(bf16[128,128]{1,0:T(8,128)(2,1)S(1)} %bitcast.13, bf16[512,512]{1,0:T(8,128)(2,1)S(1)} %copy-done.2), custom_call_target="tpu_custom_call" | custom-call | flops 67108864 | bytes 2097152 | tf_op jit(solution)/shard_map/pallas_call | solution.py:259
Async XLA Ops:
  1.4 15.8 %copy-start.3 = (bf16[512,512]{1,0:T(8,128)(2,1)S(1)}, bf16[512,512]{1,0:T(8,128)(2,1)}, u32[]{:S(2)}) copy-start(bf16[512,512]{1,0:T(8,128)(2,1)} %constant.10.clone.table) | copy-start | bytes 1572868
  1.4 15.8 %collective-permute-start = (bf16[8,4096]{1,0:T(8,128)(2,1)S(1)}, bf16[8,4096]{1,0:T(8,128)(2,1)S(1)}, u32[]{:S(2)}, u32[]{:S(2)}) collective-permute-start(bf16[8,4096]{1,0:T(8,128)(2,1)S(1)} %get-tuple-element.12), channel_id=1, source_target_pairs={{1,0},{2,1},{3,2},{4,3},{5,4},{6,5},{7,6},{8,7},{9,8},{10,9},{11,1... | collective-permute-start | bytes 196616 | tf_op jit(solution)/shard_map/ppermute | solution.py:301
  17.2 27.2 %copy-start.1 = (bf16[512,1024]{1,0:T(8,128)(2,1)S(1)}, bf16[512,1024]{1,0:T(8,128)(2,1)}, u32[]{:S(2)}) copy-start(bf16[512,1024]{1,0:T(8,128)(2,1)} %constant.11.clone.table) | copy-start | bytes 3145732
  18.5 25.9 %all-to-all-start = ((bf16[64,8,256]{2,1,0:T(8,128)(2,1)}), bf16[64,8,256]{2,1,0:T(8,128)(2,1)S(1)}, u32[]{:S(2)}, u32[]{:S(2)}) async-start(bf16[64,8,256]{2,1,0:T(8,128)(2,1)} %bitcast.3), calls=%async_computation | async-start | bytes 524288 | tf_op jit(solution)/shard_map/all_to_all | solution.py:271
  29.0 11.6 %collective-permute-start.1 = (f32[8,512]{1,0:T(8,128)S(1)}, f32[8,512]{1,0:T(8,128)S(1)}, u32[]{:S(2)}, u32[]{:S(2)}) collective-permute-start(f32[8,512]{1,0:T(8,128)S(1)} %get-tuple-element.17), channel_id=1, source_target_pairs={{0,63},{1,62},{2,61},{3,60},{4,59},{5,58},{6,57},{7,56},{8,55},{9,... | collective-permute-start | bytes 49160 | tf_op jit(solution)/shard_map/ppermute | solution.py:327
  31.5 8.2 %collective-permute-start.2 = (f32[2,512]{1,0:T(2,128)S(1)}, f32[2,512]{1,0:T(2,128)S(1)}, u32[]{:S(2)}, u32[]{:S(2)}) collective-permute-start(f32[2,512]{1,0:T(2,128)S(1)} %get-tuple-element.18), channel_id=1, source_target_pairs={{1,0},{2,1},{3,2},{4,3},{5,4},{6,5},{7,6},{8,7},{9,8},{10,9},{11,1... | collective-permute-start | bytes 12296 | tf_op jit(solution)/shard_map/ppermute | solution.py:328
  44.4 10.3 %copy-start = (bf16[1024,512]{1,0:T(8,128)(2,1)S(1)}, bf16[1024,512]{1,0:T(8,128)(2,1)}, u32[]{:S(2)}) copy-start(bf16[1024,512]{1,0:T(8,128)(2,1)} %constant.13.clone.table) | copy-start | bytes 3145732
  45.0 9.8 %copy-start.4 = (bf16[256,256]{1,0:T(8,128)(2,1)S(1)}, bf16[256,256]{1,0:T(8,128)(2,1)}, u32[]{:S(2)}) copy-start(bf16[256,256]{1,0:T(8,128)(2,1)} %constant.12.clone.spread) | copy-start | bytes 393220
  54.7 19.0 %copy-start.2 = (bf16[512,512]{1,0:T(8,128)(2,1)S(1)}, bf16[512,512]{1,0:T(8,128)(2,1)}, u32[]{:S(2)}) copy-start(bf16[512,512]{1,0:T(8,128)(2,1)} %constant.14.clone.table) | copy-start | bytes 1572868

commit v6 on v5

--- a/solution.py
+++ b/solution.py
@@ -12,9 +12,9 @@
 MARK = 64.0
 TILES = 64
 HALF = TILES // 2
-FIRST_ORDER = [(i + 60) % TILES for i in range(TILES)]
+FIRST_ORDER = [(x + 3) % 4 * 16 + (z + 12) % 16 for x in range(4) for z in range(16)]
 FRACTION_ORDER = [(i + 5) % 8 for i in range(8)]
-LAST_ORDER = [(i + 40) % TILES for i in range(TILES)]
+LAST_ORDER = [(x + 2) % 4 * 16 + (z + 8) % 16 for x in range(4) for z in range(16)]
 FRACS = 8
 COLS = 8
 ROWS = 32

time: 75 us -> 74.6 us (level)
  the two profiles are of different devices: /device:TPU:16 before, /device:TPU:20 now
where the time goes in v6:
time: 74.6 us; the launch traced here: 74.2 us
  blocking collectives  29 us (39%)
  starting transfers between devices  26.9 us (36%)
  waiting for transfers between devices  11.5 us (15%)
  Pallas kernels  6.75 us (9%)
    all_to_all x2, blocking collectives, exchange(): lax.all_to_all(blocks, axis, 0, 0, axis_index_groups=[order], tiled=True)  29 us
    ppermute x1, starting transfers between devices, per_device(): lax.ppermute(sent, 'tile', [((t + 1) % TILES, t) for t in range(TILES)])  11.5 us
    all_to_all x1, starting transfers between devices, exchange(): lax.all_to_all(blocks, axis, 0, 0, axis_index_groups=[order], tiled=True)  11.5 us
    ppermute x1, waiting for transfers between devices, per_device(): lax.ppermute(mirror, 'tile', [(t, TILES - 1 - t) for t in range(TILES)])  8.81 us
    pallas_call x6, Pallas kernels, call(): pl.pallas_call(kernel, out_shape=outs, in_specs=[block] * blocks + [pl.Bl...  6.75 us
    ppermute x1, starting transfers between devices, per_device(): lax.ppermute(mirror, 'tile', [(t, TILES - 1 - t) for t in range(TILES)])  3.25 us
    all_to_all x1, waiting for transfers between devices, exchange(): lax.all_to_all(blocks, axis, 0, 0, axis_index_groups=[order], tiled=True)  2.7 us
  transfers between devices with their start and end apart: 4, of which 2 were waited for; matrix products, arithmetic and copies ran while one was open for 0% of the time, Pallas kernels for 3%

profile of v6, /device:TPU:20, one launch (start us, length us, event | category | flops | bytes accessed | tf_op | source)
XLA Modules:
  0.0 74.2 jit_solution(11444755746769769026)
XLA Ops:
  0.0 1.4 %shard_map.109 = (bf16[8,4096]{1,0:T(8,128)(2,1)S(1)}, bf16[32,4096]{1,0:T(8,128)(2,1)S(1)}) custom-call(s32[1,512]{1,0:T(1,128)} %bitcast.16, s32[1,512]{1,0:T(1,128)} %bitcast.17, bf16[32,4096]{1,0:T(8,128)(2,1)} %bitcast.14, bf16[32,4096]{1,0:T(8,128)(2,1)} %gain_in.3), custom_call_target="tpu_custom_call" | custom-call | flops 134217728 | bytes 2097152 | tf_op jit(solution)/shard_map/pallas_call | solution.py:259
  1.4 0.0 copy-start.3
  1.4 11.5 %collective-permute-start = (bf16[8,4096]{1,0:T(8,128)(2,1)S(1)}, bf16[8,4096]{1,0:T(8,128)(2,1)S(1)}, u32[]{:S(2)}, u32[]{:S(2)}) collective-permute-start(bf16[8,4096]{1,0:T(8,128)(2,1)S(1)} %get-tuple-element.12), channel_id=1, source_target_pairs={{1,0},{2,1},{3,2},{4,3},{5,4},{6,5},{7,6},{8,7},{9,8},{10,9},{11,1... | collective-permute-start | bytes 196616 | tf_op jit(solution)/shard_map/ppermute | solution.py:301
  12.9 2.1 %shard_map.110 = (bf16[256,512]{1,0:T(8,128)(2,1)S(1)}, bf16[16,4096]{1,0:T(8,128)(2,1)S(1)}, f32[8,512]{1,0:T(8,128)S(1)}, f32[8,512]{1,0:T(8,128)S(1)}, f32[2,512]{1,0:T(2,128)S(1)}) custom-call(bf16[32,4096]{1,0:T(8,128)(2,1)S(1)} %get-tuple-element.13.fill_map, s32[8]{0:T(128)} %groups_in.1, f32[8,8,512]{2,1,0:T(8,128)} %filters_in.1, ...), custom_call_target="tpu_custom_call" | custom-call | flops 134217728 | bytes 2097152 | tf_op jit(solution)/shard_map/pallas_call | solution.py:259
  15.0 0.0 copy-start.1
  15.0 0.0 collective-permute-done.following
  15.0 0.0 copy-done.3
  15.0 1.2 %shard_map.111 = bf16[512,256]{1,0:T(8,128)(2,1)} custom-call(bf16[8,4096]{1,0:T(8,128)(2,1)S(1)} %collective-permute-done.following, bf16[256,512]{1,0:T(8,128)(2,1)S(1)} %get-tuple-element.14.filled, bf16[16,4096]{1,0:T(8,128)(2,1)S(1)} %get-tuple-element.15.tail, bf16[512,512]{1,0:T(8,128)(2,1)S(1)} %copy-done.3), custom_call_target="tpu_custom_call" | custom-call | flops 134217728 | bytes 2097152 | tf_op jit(solution)/shard_map/pallas_call | solution.py:259
  16.2 11.5 %all-to-all-start = ((bf16[64,8,256]{2,1,0:T(8,128)(2,1)}), bf16[64,8,256]{2,1,0:T(8,128)(2,1)S(1)}, u32[]{:S(2)}, u32[]{:S(2)}) async-start(bf16[64,8,256]{2,1,0:T(8,128)(2,1)} %bitcast.3), calls=%async_computation | async-start | bytes 524288 | tf_op jit(solution)/shard_map/all_to_all | solution.py:271
  27.7 3.3 %collective-permute-start.1 = (f32[8,512]{1,0:T(8,128)S(1)}, f32[8,512]{1,0:T(8,128)S(1)}, u32[]{:S(2)}, u32[]{:S(2)}) collective-permute-start(f32[8,512]{1,0:T(8,128)S(1)} %get-tuple-element.17), channel_id=1, source_target_pairs={{0,63},{1,62},{2,61},{3,60},{4,59},{5,58},{6,57},{7,56},{8,55},{9,... | collective-permute-start | bytes 49160 | tf_op jit(solution)/shard_map/ppermute | solution.py:327
  31.0 0.7 collective-permute-start.2
  31.6 0.0 collective-permute-done.2.following
  31.7 8.8 %collective-permute-done.1.mirror = f32[8,512]{1,0:T(8,128)S(1)} collective-permute-done((f32[8,512]{1,0:T(8,128)S(1)}, f32[8,512]{1,0:T(8,128)S(1)}, u32[]{:S(2)}, u32[]{:S(2)}) %collective-permute-start.1) | collective-permute-done | bytes 16416 | tf_op jit(solution)/shard_map/ppermute | solution.py:327
  40.5 2.7 %all-to-all-done = bf16[64,8,256]{2,1,0:T(8,128)(2,1)S(1)} async-done(((bf16[64,8,256]{2,1,0:T(8,128)(2,1)}), bf16[64,8,256]{2,1,0:T(8,128)(2,1)S(1)}, u32[]{:S(2)}, u32[]{:S(2)}) %all-to-all-start) | async-done | bytes 262176 | tf_op jit(solution)/shard_map/all_to_all | solution.py:271
  43.2 0.0 copy-done.1
  43.2 0.0 copy-start
  43.2 0.6 shard_map.112
  43.8 0.0 copy-start.4
  43.8 9.7 %all_to_all.15 = bf16[8,32,512]{2,1,0:T(8,128)(2,1)S(1)} all-to-all(bf16[8,32,512]{2,1,0:T(8,128)(2,1)S(1)} %bitcast.10), channel_id=1, replica_groups={{320,384,448,0,64,128,192,256},{321,385,449,1,65,129,193,257},{322,386,..., dimensions={0} | all-to-all | bytes 524288 | tf_op jit(solution)/shard_map/all_to_all | solution.py:271
  53.5 0.0 copy-done
  53.5 0.0 copy-done.4
  53.5 0.0 copy-start.2
  53.5 0.6 shard_map.113
  54.2 19.2 %all_to_all.16 = bf16[64,2,128]{2,1,0:T(2,128)(2,1)S(1)} all-to-all(bf16[64,2,128]{2,1,0:T(2,128)(2,1)S(1)} %bitcast.12), channel_id=1, replica_groups={{40,41,42,43,44,45,46,47,32,33,34,35,36,37,38,39,56,57,58,59,60,61,62,6..., dimensions={0} | all-to-all | bytes 65536 | tf_op jit(solution)/shard_map/all_to_all | solution.py:271
  73.4 0.0 copy-done.2
  73.4 0.9 %shard_map.114 = f32[4,8,512]{2,1,0:T(8,128)} custom-call(bf16[128,128]{1,0:T(8,128)(2,1)S(1)} %bitcast.13, bf16[512,512]{1,0:T(8,128)(2,1)S(1)} %copy-done.2), custom_call_target="tpu_custom_call" | custom-call | flops 67108864 | bytes 2097152 | tf_op jit(solution)/shard_map/pallas_call | solution.py:259
Async XLA Ops:
  1.4 13.6 %copy-start.3 = (bf16[512,512]{1,0:T(8,128)(2,1)S(1)}, bf16[512,512]{1,0:T(8,128)(2,1)}, u32[]{:S(2)}) copy-start(bf16[512,512]{1,0:T(8,128)(2,1)} %constant.10.clone.table) | copy-start | bytes 1572868
  1.4 13.6 %collective-permute-start = (bf16[8,4096]{1,0:T(8,128)(2,1)S(1)}, bf16[8,4096]{1,0:T(8,128)(2,1)S(1)}, u32[]{:S(2)}, u32[]{:S(2)}) collective-permute-start(bf16[8,4096]{1,0:T(8,128)(2,1)S(1)} %get-tuple-element.12), channel_id=1, source_target_pairs={{1,0},{2,1},{3,2},{4,3},{5,4},{6,5},{7,6},{8,7},{9,8},{10,9},{11,1... | collective-permute-start | bytes 196616 | tf_op jit(solution)/shard_map/ppermute | solution.py:301
  15.0 28.2 %copy-start.1 = (bf16[512,1024]{1,0:T(8,128)(2,1)S(1)}, bf16[512,1024]{1,0:T(8,128)(2,1)}, u32[]{:S(2)}) copy-start(bf16[512,1024]{1,0:T(8,128)(2,1)} %constant.11.clone.table) | copy-start | bytes 3145732
  16.2 26.9 %all-to-all-start = ((bf16[64,8,256]{2,1,0:T(8,128)(2,1)}), bf16[64,8,256]{2,1,0:T(8,128)(2,1)S(1)}, u32[]{:S(2)}, u32[]{:S(2)}) async-start(bf16[64,8,256]{2,1,0:T(8,128)(2,1)} %bitcast.3), calls=%async_computation | async-start | bytes 524288 | tf_op jit(solution)/shard_map/all_to_all | solution.py:271
  27.7 12.8 %collective-permute-start.1 = (f32[8,512]{1,0:T(8,128)S(1)}, f32[8,512]{1,0:T(8,128)S(1)}, u32[]{:S(2)}, u32[]{:S(2)}) collective-permute-start(f32[8,512]{1,0:T(8,128)S(1)} %get-tuple-element.17), channel_id=1, source_target_pairs={{0,63},{1,62},{2,61},{3,60},{4,59},{5,58},{6,57},{7,56},{8,55},{9,... | collective-permute-start | bytes 49160 | tf_op jit(solution)/shard_map/ppermute | solution.py:327
  31.0 0.7 collective-permute-start.2
  43.2 10.3 %copy-start = (bf16[1024,512]{1,0:T(8,128)(2,1)S(1)}, bf16[1024,512]{1,0:T(8,128)(2,1)}, u32[]{:S(2)}) copy-start(bf16[1024,512]{1,0:T(8,128)(2,1)} %constant.13.clone.table) | copy-start | bytes 3145732
  43.8 9.8 %copy-start.4 = (bf16[256,256]{1,0:T(8,128)(2,1)S(1)}, bf16[256,256]{1,0:T(8,128)(2,1)}, u32[]{:S(2)}) copy-start(bf16[256,256]{1,0:T(8,128)(2,1)} %constant.12.clone.spread) | copy-start | bytes 393220
  53.5 19.9 %copy-start.2 = (bf16[512,512]{1,0:T(8,128)(2,1)S(1)}, bf16[512,512]{1,0:T(8,128)(2,1)}, u32[]{:S(2)}) copy-start(bf16[512,512]{1,0:T(8,128)(2,1)} %constant.14.clone.table) | copy-start | bytes 1572868

commit v7 on v6

--- a/solution.py
+++ b/solution.py
@@ -224,10 +224,10 @@
                 by_row[row, :, 384:] = jnp.where(wraps, found[(a - 1) % 4 * 4 + 3], found[a * 4 + 3])
     operand = by_row[...].reshape(256, N).astype(BF16)
     scale = pair[...][None]
+    signed = jnp.where(lax.broadcasted_iota(jnp.int32, (1, 8, 1), 1) < 4, -scale, scale)
     with_cosine = dot(operand, table[:, :N], (1, 0)).reshape(32, 8, N) * scale
-    with_sine = dot(operand, table[:, N:], (1, 0)).reshape(32, 8, N) * scale
-    sign = jnp.where(lax.broadcasted_iota(jnp.int32, (1, 8, 1), 1) < 4, 1.0, -1.0)
-    total = with_cosine + sign * pltpu.roll(with_sine, 4, 1)
+    with_sine = dot(operand, table[:, N:], (1, 0)).reshape(32, 8, N) * signed
+    total = with_cosine + pltpu.roll(with_sine, 4, 1)
     out[...] = total.reshape(256, N).astype(BF16)
 
 

time: 74.6 us -> 74.6 us (level)
  no operation moved by 1% of the time
where the time goes in v7:
time: 74.6 us; the launch traced here: 74.2 us
  blocking collectives  28.9 us (39%)
  starting transfers between devices  26.9 us (36%)
  waiting for transfers between devices  11.5 us (15%)
  Pallas kernels  6.75 us (9%)
    all_to_all x2, blocking collectives, exchange(): lax.all_to_all(blocks, axis, 0, 0, axis_index_groups=[order], tiled=True)  28.9 us
    ppermute x1, starting transfers between devices, per_device(): lax.ppermute(sent, 'tile', [((t + 1) % TILES, t) for t in range(TILES)])  11.5 us
    all_to_all x1, starting transfers between devices, exchange(): lax.all_to_all(blocks, axis, 0, 0, axis_index_groups=[order], tiled=True)  11.5 us
    ppermute x1, waiting for transfers between devices, per_device(): lax.ppermute(mirror, 'tile', [(t, TILES - 1 - t) for t in range(TILES)])  8.81 us
    pallas_call x6, Pallas kernels, call(): pl.pallas_call(kernel, out_shape=outs, in_specs=[block] * blocks + [pl.Bl...  6.75 us
    ppermute x1, starting transfers between devices, per_device(): lax.ppermute(mirror, 'tile', [(t, TILES - 1 - t) for t in range(TILES)])  3.25 us
    all_to_all x1, waiting for transfers between devices, exchange(): lax.all_to_all(blocks, axis, 0, 0, axis_index_groups=[order], tiled=True)  2.7 us
  transfers between devices with their start and end apart: 4, of which 2 were waited for; matrix products, arithmetic and copies ran while one was open for 0% of the time, Pallas kernels for 3%

profile of v7, /device:TPU:20, one launch (start us, length us, event | category | flops | bytes accessed | tf_op | source)
XLA Modules:
  0.0 74.2 jit_solution(18182613831956047623)
XLA Ops:
  0.0 1.4 %shard_map.109 = (bf16[8,4096]{1,0:T(8,128)(2,1)S(1)}, bf16[32,4096]{1,0:T(8,128)(2,1)S(1)}) custom-call(s32[1,512]{1,0:T(1,128)} %bitcast.16, s32[1,512]{1,0:T(1,128)} %bitcast.17, bf16[32,4096]{1,0:T(8,128)(2,1)} %bitcast.14, bf16[32,4096]{1,0:T(8,128)(2,1)} %gain_in.3), custom_call_target="tpu_custom_call" | custom-call | flops 134217728 | bytes 2097152 | tf_op jit(solution)/shard_map/pallas_call | solution.py:259
  1.4 0.0 copy-start.3
  1.4 11.5 %collective-permute-start = (bf16[8,4096]{1,0:T(8,128)(2,1)S(1)}, bf16[8,4096]{1,0:T(8,128)(2,1)S(1)}, u32[]{:S(2)}, u32[]{:S(2)}) collective-permute-start(bf16[8,4096]{1,0:T(8,128)(2,1)S(1)} %get-tuple-element.12), channel_id=1, source_target_pairs={{1,0},{2,1},{3,2},{4,3},{5,4},{6,5},{7,6},{8,7},{9,8},{10,9},{11,1... | collective-permute-start | bytes 196616 | tf_op jit(solution)/shard_map/ppermute | solution.py:301
  12.9 2.1 %shard_map.110 = (bf16[256,512]{1,0:T(8,128)(2,1)S(1)}, bf16[16,4096]{1,0:T(8,128)(2,1)S(1)}, f32[8,512]{1,0:T(8,128)S(1)}, f32[8,512]{1,0:T(8,128)S(1)}, f32[2,512]{1,0:T(2,128)S(1)}) custom-call(bf16[32,4096]{1,0:T(8,128)(2,1)S(1)} %get-tuple-element.13.fill_map, s32[8]{0:T(128)} %groups_in.1, f32[8,8,512]{2,1,0:T(8,128)} %filters_in.1, ...), custom_call_target="tpu_custom_call" | custom-call | flops 134217728 | bytes 2097152 | tf_op jit(solution)/shard_map/pallas_call | solution.py:259
  15.0 0.0 copy-start.1
  15.0 0.0 collective-permute-done.following
  15.0 0.0 copy-done.3
  15.0 1.2 %shard_map.111 = bf16[512,256]{1,0:T(8,128)(2,1)} custom-call(bf16[8,4096]{1,0:T(8,128)(2,1)S(1)} %collective-permute-done.following, bf16[256,512]{1,0:T(8,128)(2,1)S(1)} %get-tuple-element.14.filled, bf16[16,4096]{1,0:T(8,128)(2,1)S(1)} %get-tuple-element.15.tail, bf16[512,512]{1,0:T(8,128)(2,1)S(1)} %copy-done.3), custom_call_target="tpu_custom_call" | custom-call | flops 134217728 | bytes 2097152 | tf_op jit(solution)/shard_map/pallas_call | solution.py:259
  16.2 11.5 %all-to-all-start = ((bf16[64,8,256]{2,1,0:T(8,128)(2,1)}), bf16[64,8,256]{2,1,0:T(8,128)(2,1)S(1)}, u32[]{:S(2)}, u32[]{:S(2)}) async-start(bf16[64,8,256]{2,1,0:T(8,128)(2,1)} %bitcast.3), calls=%async_computation | async-start | bytes 524288 | tf_op jit(solution)/shard_map/all_to_all | solution.py:271
  27.7 3.3 %collective-permute-start.1 = (f32[8,512]{1,0:T(8,128)S(1)}, f32[8,512]{1,0:T(8,128)S(1)}, u32[]{:S(2)}, u32[]{:S(2)}) collective-permute-start(f32[8,512]{1,0:T(8,128)S(1)} %get-tuple-element.17), channel_id=1, source_target_pairs={{0,63},{1,62},{2,61},{3,60},{4,59},{5,58},{6,57},{7,56},{8,55},{9,... | collective-permute-start | bytes 49160 | tf_op jit(solution)/shard_map/ppermute | solution.py:327
  31.0 0.7 collective-permute-start.2
  31.6 0.0 collective-permute-done.2.following
  31.7 8.8 %collective-permute-done.1.mirror = f32[8,512]{1,0:T(8,128)S(1)} collective-permute-done((f32[8,512]{1,0:T(8,128)S(1)}, f32[8,512]{1,0:T(8,128)S(1)}, u32[]{:S(2)}, u32[]{:S(2)}) %collective-permute-start.1) | collective-permute-done | bytes 16416 | tf_op jit(solution)/shard_map/ppermute | solution.py:327
  40.5 2.7 %all-to-all-done = bf16[64,8,256]{2,1,0:T(8,128)(2,1)S(1)} async-done(((bf16[64,8,256]{2,1,0:T(8,128)(2,1)}), bf16[64,8,256]{2,1,0:T(8,128)(2,1)S(1)}, u32[]{:S(2)}, u32[]{:S(2)}) %all-to-all-start) | async-done | bytes 262176 | tf_op jit(solution)/shard_map/all_to_all | solution.py:271
  43.2 0.0 copy-done.1
  43.2 0.0 copy-start
  43.2 0.6 shard_map.112
  43.7 0.0 copy-start.4
  43.8 9.7 %all_to_all.15 = bf16[8,32,512]{2,1,0:T(8,128)(2,1)S(1)} all-to-all(bf16[8,32,512]{2,1,0:T(8,128)(2,1)S(1)} %bitcast.10), channel_id=1, replica_groups={{320,384,448,0,64,128,192,256},{321,385,449,1,65,129,193,257},{322,386,..., dimensions={0} | all-to-all | bytes 524288 | tf_op jit(solution)/shard_map/all_to_all | solution.py:271
  53.5 0.0 copy-done
  53.5 0.0 copy-done.4
  53.5 0.0 copy-start.2
  53.5 0.6 shard_map.113
  54.2 19.2 %all_to_all.16 = bf16[64,2,128]{2,1,0:T(2,128)(2,1)S(1)} all-to-all(bf16[64,2,128]{2,1,0:T(2,128)(2,1)S(1)} %bitcast.12), channel_id=1, replica_groups={{40,41,42,43,44,45,46,47,32,33,34,35,36,37,38,39,56,57,58,59,60,61,62,6..., dimensions={0} | all-to-all | bytes 65536 | tf_op jit(solution)/shard_map/all_to_all | solution.py:271
  73.4 0.0 copy-done.2
  73.4 0.9 %shard_map.114 = f32[4,8,512]{2,1,0:T(8,128)} custom-call(bf16[128,128]{1,0:T(8,128)(2,1)S(1)} %bitcast.13, bf16[512,512]{1,0:T(8,128)(2,1)S(1)} %copy-done.2), custom_call_target="tpu_custom_call" | custom-call | flops 67108864 | bytes 2097152 | tf_op jit(solution)/shard_map/pallas_call | solution.py:259
Async XLA Ops:
  1.4 13.6 %copy-start.3 = (bf16[512,512]{1,0:T(8,128)(2,1)S(1)}, bf16[512,512]{1,0:T(8,128)(2,1)}, u32[]{:S(2)}) copy-start(bf16[512,512]{1,0:T(8,128)(2,1)} %constant.10.clone.table) | copy-start | bytes 1572868
  1.4 13.6 %collective-permute-start = (bf16[8,4096]{1,0:T(8,128)(2,1)S(1)}, bf16[8,4096]{1,0:T(8,128)(2,1)S(1)}, u32[]{:S(2)}, u32[]{:S(2)}) collective-permute-start(bf16[8,4096]{1,0:T(8,128)(2,1)S(1)} %get-tuple-element.12), channel_id=1, source_target_pairs={{1,0},{2,1},{3,2},{4,3},{5,4},{6,5},{7,6},{8,7},{9,8},{10,9},{11,1... | collective-permute-start | bytes 196616 | tf_op jit(solution)/shard_map/ppermute | solution.py:301
  15.0 28.2 %copy-start.1 = (bf16[512,1024]{1,0:T(8,128)(2,1)S(1)}, bf16[512,1024]{1,0:T(8,128)(2,1)}, u32[]{:S(2)}) copy-start(bf16[512,1024]{1,0:T(8,128)(2,1)} %constant.11.clone.table) | copy-start | bytes 3145732
  16.2 26.9 %all-to-all-start = ((bf16[64,8,256]{2,1,0:T(8,128)(2,1)}), bf16[64,8,256]{2,1,0:T(8,128)(2,1)S(1)}, u32[]{:S(2)}, u32[]{:S(2)}) async-start(bf16[64,8,256]{2,1,0:T(8,128)(2,1)} %bitcast.3), calls=%async_computation | async-start | bytes 524288 | tf_op jit(solution)/shard_map/all_to_all | solution.py:271
  27.7 12.8 %collective-permute-start.1 = (f32[8,512]{1,0:T(8,128)S(1)}, f32[8,512]{1,0:T(8,128)S(1)}, u32[]{:S(2)}, u32[]{:S(2)}) collective-permute-start(f32[8,512]{1,0:T(8,128)S(1)} %get-tuple-element.17), channel_id=1, source_target_pairs={{0,63},{1,62},{2,61},{3,60},{4,59},{5,58},{6,57},{7,56},{8,55},{9,... | collective-permute-start | bytes 49160 | tf_op jit(solution)/shard_map/ppermute | solution.py:327
  31.0 0.7 collective-permute-start.2
  43.2 10.3 %copy-start = (bf16[1024,512]{1,0:T(8,128)(2,1)S(1)}, bf16[1024,512]{1,0:T(8,128)(2,1)}, u32[]{:S(2)}) copy-start(bf16[1024,512]{1,0:T(8,128)(2,1)} %constant.13.clone.table) | copy-start | bytes 3145732
  43.7 9.8 %copy-start.4 = (bf16[256,256]{1,0:T(8,128)(2,1)S(1)}, bf16[256,256]{1,0:T(8,128)(2,1)}, u32[]{:S(2)}) copy-start(bf16[256,256]{1,0:T(8,128)(2,1)} %constant.12.clone.spread) | copy-start | bytes 393220
  53.5 19.9 %copy-start.2 = (bf16[512,512]{1,0:T(8,128)(2,1)S(1)}, bf16[512,512]{1,0:T(8,128)(2,1)}, u32[]{:S(2)}) copy-start(bf16[512,512]{1,0:T(8,128)(2,1)} %constant.14.clone.table) | copy-start | bytes 1572868
